TPU v7x, 32 devices: a whole 2x2x4 slice. The times are simulated.
32 devices in a mesh: src: 4 (over z), vol: 8 (over y, x, core).
Axes of the slice: x: 2, y: 2, z: 4, core: 2. Of those that a mesh axis runs over, the one named last changes fastest.
Arguments:
- forward: bfloat16 [4096, 36, 512], P(('src', 'vol')), may hold values from -6 to 6
- item_tx: int32 [4096], P(('src', 'vol')), may hold values from 0 to 15, as said below
- item_brick: int32 [4096], P(('src', 'vol')), may hold values from 0 to 255
- tx_place: int32 [16], replicated, may hold values from 0 to 15, as said below
- brick_place: int32 [256], replicated, may hold values from 0 to 255, as said below
- adjoint: bfloat16 [16, 256, 36, 512], P('src', 'vol'), may hold values from -6 to 6
Outputs:
- gradient: float32 [2, 64, 16, 128], P(None, 'vol')
Inputs may be any that keep to these rules, and one draw needn't show every extreme that they name: Stored brick i goes to owner (tx_place[item_tx[i]] // 4, brick_place[item_brick[i]] // 32) as (src index, vol index). Among the stored bricks of one device at most 8 share an owner; in every draw one owner receives exactly 8 from every device. `tx_place`: A permutation. `brick_place`: A permutation.
All inputs are finite; a program needn't handle non-finite values.
Results may differ from a plain program's by a relative error of at most 0.0003.
Values may be sent and summed in bfloat16 or wider, within the bound.
A program may use at most 128 MiB of HBM per device.

v0:
```python
import math

import jax
import jax.numpy as jnp
from jax import lax
from jax.sharding import PartitionSpec as P

E = 8
NFREQ = 6
NBY = 2
NBZ = 16


def with_halo(cells, sides, width):
    for axis, dim in sides:
        count = lax.axis_size(axis)
        ends = count - 1
        head = lax.slice_in_dim(cells, 0, width, axis=dim)
        tail = lax.slice_in_dim(cells, cells.shape[dim] - width, cells.shape[dim], axis=dim)
        cells = jnp.concatenate(
            [
                lax.ppermute(tail, axis, [(i, (i + 1) % count) for i in range(ends)]),
                cells,
                lax.ppermute(head, axis, [((i + 1) % count, i) for i in range(ends)]),
            ],
            axis=dim,
        )
    return cells


def tap_weights():
    raw_taps = [math.exp(-(offset - 4) * (offset - 4) / 4.5) for offset in range(9)]
    tap_total = sum(raw_taps)
    return [tap_value / tap_total for tap_value in raw_taps]


def correlate(fwd_field, adj_field):
    lead_shape = fwd_field.shape[:-2]
    fwd_split = fwd_field.reshape(lead_shape + (NFREQ, 3, 2, fwd_field.shape[-1]))
    adj_split = adj_field.reshape(lead_shape + (NFREQ, 3, 2, adj_field.shape[-1]))
    products = (
        fwd_split[..., 0, :] * adj_split[..., 0, :] - fwd_split[..., 1, :] * adj_split[..., 1, :]
    )
    horizontal = jnp.sum(products[..., 0:2, :], axis=(-3, -2))
    vertical = jnp.sum(products[..., 2, :], axis=-2)
    return jnp.stack([horizontal, vertical], axis=-2)


def smooth_axis(padded, axis):
    weights = tap_weights()
    length = padded.shape[axis] - 8
    summed = jnp.zeros(padded.shape[:axis] + (length,) + padded.shape[axis + 1 :], jnp.float32)
    for offset in range(9):
        summed = summed + weights[offset] * lax.slice_in_dim(
            padded, offset, offset + length, axis=axis
        )
    return summed


def pad_axis(field, axis):
    widths = [(0, 0)] * field.ndim
    widths[axis] = (4, 4)
    return jnp.pad(field, widths)


def lookup(indices, table):
    hits = indices[:, None] == jnp.arange(table.shape[0], dtype=jnp.int32)[None, :]
    return jnp.sum(jnp.where(hits, table[None, :], 0), axis=1)


def local(forward, item_tx, item_brick, tx_place, brick_place, adjoint):
    stored = forward.shape[0]
    channels = forward.shape[1]
    cells = forward.shape[2]
    src_count = lax.axis_size("src")
    vol_count = lax.axis_size("vol")
    devices = src_count * vol_count
    local_tx = adjoint.shape[0]
    local_bricks = adjoint.shape[1]
    capacity = max(2, 2 * stored // devices)
    slot_total = devices * capacity
    tx_at = lookup(item_tx, tx_place)
    brick_at = lookup(item_brick, brick_place)
    destination = tx_at // local_tx * vol_count + brick_at // local_bricks
    pair_index = tx_at % local_tx * local_bricks + brick_at % local_bricks
    positions = jnp.arange(stored, dtype=jnp.int32)
    same_owner = destination[:, None] == destination[None, :]
    earlier = positions[:, None] > positions[None, :]
    order_rank = jnp.sum((same_owner & earlier).astype(jnp.int32), axis=1)
    slot_index = destination * capacity + order_rank
    outgoing = jnp.zeros((slot_total, channels, cells), forward.dtype).at[slot_index].set(forward)
    slot_pairs = jnp.full((slot_total,), -1, jnp.int32).at[slot_index].set(pair_index)
    arrived, arrived_pairs = (
        lax.all_to_all(outgoing, ("src", "vol"), split_axis=0, concat_axis=0, tiled=True),
        lax.all_to_all(slot_pairs, ("src", "vol"), split_axis=0, concat_axis=0, tiled=True),
    )
    filled = arrived_pairs >= 0
    flat_adjoint = adjoint.reshape(local_tx * local_bricks, channels, cells)
    picked = flat_adjoint[jnp.maximum(arrived_pairs, 0)]
    product = correlate(arrived.astype(jnp.float32), picked.astype(jnp.float32))
    owner_brick = arrived_pairs % local_bricks
    owner_table = (
        (owner_brick[None, :] == jnp.arange(local_bricks, dtype=jnp.int32)[:, None])
        & filled[None, :]
    ).astype(jnp.float32)
    gradient = jnp.dot(
        owner_table, product.reshape(slot_total, 2 * cells), precision=lax.Precision.HIGHEST
    )
    gradient = gradient.reshape(local_bricks, 2, cells)
    slab = (
        gradient.reshape(NBY, NBZ, 2, E, E, E)
        .transpose(2, 3, 0, 4, 1, 5)
        .reshape(2, E, NBY * E, NBZ * E)
    )
    summed = lax.psum(slab, "src")
    padded = with_halo(summed, (("vol", 1),), 4)
    field = smooth_axis(padded, 1)
    for axis in (2, 3):
        field = smooth_axis(pad_axis(field, axis), axis)
    return field


def solution(mesh):
    in_specs = (
        P(("src", "vol"), None, None),
        P(("src", "vol")),
        P(("src", "vol")),
        P(),
        P(),
        P("src", "vol", None, None),
    )
    out_specs = P(None, "vol", None, None)
    return jax.shard_map(local, mesh=mesh, in_specs=in_specs, out_specs=out_specs, check_vma=False)
```

profile of v0, /device:TPU:3, one launch (start us, length us, event | category | flops | bytes accessed | tf_op | source)
XLA Modules:
  0.0 379.1 jit_solution(14258543499984967538)
XLA Ops:
  8.4 1.0 scatter_custom_fusion
  10.1 6.4 %all-to-all-start = ((s32[32,8,1]{1,2,0:T(1,128)}), s32[32,8,1]{1,2,0:T(1,128)S(1)}, u32[]{:S(2)}, u32[]{:S(2)}) async-start(s32[32,8,1]{1,2,0:T(1,128)} %bitcast.4), calls=%async_computation | async-start | bytes 32768 | tf_op jit(solution)/shard_map/all_to_all | solution.py:95
  16.5 7.3 %copy.49 = bf16[128,36,512]{2,1,0:T(8,128)(2,1)} copy(bf16[128,36,512]{2,0,1:T(8,128)(2,1)} %param.6) | data formatting | bytes 9437184 | tf_op args[0]
  23.8 4.6 %broadcast_in_dim.33 = bf16[256,36,512]{2,1,0:T(8,128)(2,1)} broadcast(bf16[]{:T(256)} %constant.77.clone.1), dimensions={} | broadcast | bytes 9437186 | tf_op jit(solution)/shard_map/broadcast_in_dim | solution.py:91
  28.4 20.6 %scatter_fusion = bf16[256,36,512]{2,1,0:T(8,128)(2,1)} fusion(bf16[256,36,512]{2,1,0:T(8,128)(2,1)} %broadcast_in_dim.33, s32[128]{0:T(128)S(1)} %fusion.52, bf16[128,36,512]{2,1,0:T(8,128)(2,1)} %copy.49), kind=kCustom, calls=%fused_computation.2 | custom fusion | bytes 14156288 | tf_op jit(solution)/shard_map/scatter | solution.py:91
  49.0 5.9 %all-to-all-start.1 = ((bf16[256,36,512]{2,1,0:T(8,128)(2,1)}), bf16[256,36,512]{2,1,0:T(8,128)(2,1)}, u32[]{:S(2)}, u32[]{:S(2)}) async-start(bf16[256,36,512]{2,1,0:T(8,128)(2,1)} %scatter_fusion), calls=%async_computation.1 | async-start | bytes 20971520 | tf_op jit(solution)/shard_map/all_to_all | solution.py:94
  54.9 2.7 copy.51
  57.6 5.1 %copy.52 = bf16[128,36,512]{2,1,0:T(8,128)(2,1)} copy(bf16[128,36,512]{2,0,1:T(8,128)(2,1)S(1)} %bitcast.58) | data formatting | bytes 9437184 | tf_op jit(solution)/shard_map/reshape | solution.py:98
  64.1 12.1 %gather_fusion = bf16[256,36,512]{2,1,0:T(8,128)(2,1)} fusion(bf16[128,36,512]{2,1,0:T(8,128)(2,1)} %copy.52, s32[1024]{0:T(1024)S(1)} %pad_clamp_fusion), kind=kCustom, calls=%fused_computation | custom fusion | bytes 18875392 | tf_op jit(solution)/shard_map/gather | solution.py:99
  76.2 10.9 %copy.53 = bf16[256,36,512]{2,0,1:T(8,128)(2,1)} copy(bf16[256,36,512]{2,1,0:T(8,128)(2,1)} %gather_fusion) | data formatting | bytes 18874368 | tf_op jit(solution)/shard_map/gather | solution.py:99
  87.1 12.7 %convert.3 = f32[256,6,3,2,512]{4,0,3,2,1:T(8,128)} convert(bf16[256,6,3,2,512]{4,0,3,2,1:T(8,128)(2,1)} %bitcast.56) | non-fusion elementwise | flops 4718592 | bytes 28311552 | tf_op jit(solution)/shard_map/convert_element_type | solution.py:100
  99.8 183.3 %all-to-all-done.1 = bf16[256,36,512]{2,1,0:T(8,128)(2,1)} async-done(((bf16[256,36,512]{2,1,0:T(8,128)(2,1)}), bf16[256,36,512]{2,1,0:T(8,128)(2,1)}, u32[]{:S(2)}, u32[]{:S(2)}) %all-to-all-start.1) | async-done | bytes 9437216 | tf_op jit(solution)/shard_map/all_to_all | solution.py:94
  283.1 10.9 %copy.50 = bf16[256,36,512]{2,0,1:T(8,128)(2,1)} copy(bf16[256,36,512]{2,1,0:T(8,128)(2,1)} %all-to-all-done.1) | data formatting | bytes 18874368 | tf_op jit(solution)/shard_map/all_to_all | solution.py:94
  294.0 12.7 %convert.2 = f32[256,6,3,2,512]{4,0,3,2,1:T(8,128)} convert(bf16[256,6,3,2,512]{4,0,3,2,1:T(8,128)(2,1)} %bitcast.57) | non-fusion elementwise | flops 4718592 | bytes 28311552 | tf_op jit(solution)/shard_map/reshape | solution.py:39
  306.7 14.0 %fusion.1 = f32[256,6,3,512]{3,0,2,1:T(8,128)S(1)} fusion(f32[256,6,3,2,512]{4,0,3,2,1:T(8,128)} %convert.3, f32[256,6,3,2,512]{4,0,3,2,1:T(8,128)} %convert.2), kind=kLoop, calls=%fused_computation.5 | loop fusion | flops 7077888 | bytes 47185920 | tf_op jit(solution)/shard_map/sub | solution.py:42
  323.6 1.6 reshape.258
  325.2 31.8 %all-reduce.4.cloned.1.call-done = f32[2,8,16,128]{3,2,1,0:T(8,128)} async-done(((f32[2,8,16,128]{3,2,1,0:T(8,128)}), f32[2,8,16,128]{3,2,1,0:T(8,128)}) %all-reduce.4.cloned.1.call-update) | async-done | bytes 131088 | tf_op jit(solution)/shard_map/psum | solution.py:115
  357.0 0.9 fusion.56
  357.9 5.7 %collective-permute-start = (f32[2,4,16,128]{3,2,1,0:T(8,128)S(1)}, f32[2,4,16,128]{3,2,1,0:T(8,128)S(1)}, u32[]{:S(2)}, u32[]{:S(2)}) collective-permute-start(f32[2,4,16,128]{3,2,1,0:T(8,128)S(1)} %get-tuple-element.9), channel_id=1, source_target_pairs={{0,1},{1,2},{2,3},{3,4},{4,5},{5,6},{6,7},{8,9},{9,10},{10,11},{11... | collective-permute-start | bytes 196616 | tf_op jit(solution)/shard_map/ppermute | solution.py:22
  363.6 1.9 collective-permute-start.1
  365.5 0.9 constant_dynamic-update-slice_fusion
  366.5 3.6 collective-permute-done.1
  370.1 1.0 fusion.34
  371.2 1.0 fusion.26
  (27 shorter events, 7.0 us)
Async XLA Ops:
  10.1 38.9 %all-to-all-start = ((s32[32,8,1]{1,2,0:T(1,128)}), s32[32,8,1]{1,2,0:T(1,128)S(1)}, u32[]{:S(2)}, u32[]{:S(2)}) async-start(s32[32,8,1]{1,2,0:T(1,128)} %bitcast.4), calls=%async_computation | async-start | bytes 32768 | tf_op jit(solution)/shard_map/all_to_all | solution.py:95
  49.0 234.2 %all-to-all-start.1 = ((bf16[256,36,512]{2,1,0:T(8,128)(2,1)}), bf16[256,36,512]{2,1,0:T(8,128)(2,1)}, u32[]{:S(2)}, u32[]{:S(2)}) async-start(bf16[256,36,512]{2,1,0:T(8,128)(2,1)} %scatter_fusion), calls=%async_computation.1 | async-start | bytes 20971520 | tf_op jit(solution)/shard_map/all_to_all | solution.py:94
  54.8 302.2 %all-reduce.4.cloned.1.call-start = ((), (), s32[]{:S(2)}) async-start(), calls=%async_computation.2 | async-start | bytes 262144 | tf_op jit(solution)/shard_map/psum | solution.py:115
  357.9 7.7 %collective-permute-start = (f32[2,4,16,128]{3,2,1,0:T(8,128)S(1)}, f32[2,4,16,128]{3,2,1,0:T(8,128)S(1)}, u32[]{:S(2)}, u32[]{:S(2)}) collective-permute-start(f32[2,4,16,128]{3,2,1,0:T(8,128)S(1)} %get-tuple-element.9), channel_id=1, source_target_pairs={{0,1},{1,2},{2,3},{3,4},{4,5},{5,6},{6,7},{8,9},{9,10},{10,11},{11... | collective-permute-start | bytes 196616 | tf_op jit(solution)/shard_map/ppermute | solution.py:22
  363.6 6.5 %collective-permute-start.1 = (f32[2,4,16,128]{3,2,1,0:T(8,128)S(1)}, f32[2,4,16,128]{3,2,1,0:T(8,128)S(1)}, u32[]{:S(2)}, u32[]{:S(2)}) collective-permute-start(f32[2,4,16,128]{3,2,1,0:T(8,128)S(1)} %get-tuple-element.10), channel_id=1, source_target_pairs={{1,0},{2,1},{3,2},{4,3},{5,4},{6,5},{7,6},{9,8},{10,9},{11,10},{12... | collective-permute-start | bytes 196616 | tf_op jit(solution)/shard_map/ppermute | solution.py:24
Sparse Core Ops, SparseCore 0:
  325.3 31.6 all-reduce.3
where the time goes:
time: 380 us; the launch traced here: 379 us
  waiting for transfers between devices  219 us (58%)
  local copies, waits for them, and re-layouts  80.8 us (21%)
  other arithmetic  45.3 us (12%)
  starting transfers between devices  20 us (5%)
  between operations  13.6 us (4%)
    all_to_all x1, waiting for transfers between devices, local(): lax.all_to_all(outgoing, ('src', 'vol'), split_axis=0, concat_axis=0, til...  183 us
    psum x1, waiting for transfers between devices, local(): summed = lax.psum(slab, 'src')  31.8 us
    gather x2, local copies, waits for them, and re-layouts, local(): picked = flat_adjoint[jnp.maximum(arrived_pairs, 0)]  23 us
    scatter x1, local copies, waits for them, and re-layouts, local(): jnp.zeros((slot_total, channels, cells), forward.dtype).at[slot_index]  20.6 us
    sub x1, other arithmetic, correlate(): fwd_split[..., 0, :] * adj_split[..., 0, :]  14 us
    convert_element_type x1, other arithmetic, local(): product = correlate(arrived.astype(jnp.float32), picked.astype(jnp.float32))  12.7 us
    reshape x1, other arithmetic, correlate(): fwd_field.reshape(lead_shape + (NFREQ, 3, 2, fwd_field.shape[-1]))  12.7 us
    all_to_all x1, local copies, waits for them, and re-layouts, local(): lax.all_to_all(outgoing, ('src', 'vol'), split_axis=0, concat_axis=0, til...  10.9 us
  transfers between devices with their start and end apart: 5, of which 3 were waited for; matrix products, arithmetic and copies ran while one was open for 21% of the time, Pallas kernels for 0%

commit v1 on v0

v1 whole, which is shorter than its diff:
```python
import functools
import math

import jax
import jax.numpy as jnp
from jax import lax
from jax.experimental import pallas as pl
from jax.experimental.pallas import tpu as pltpu
from jax.sharding import PartitionSpec as P

E = 8
NBY = 2
NBZ = 16
GROUP = 4
DIRECT = 4
SPILL = 16
PARAMS = pltpu.CompilerParams(vmem_limit_bytes=48 * 1024 * 1024)


def with_halo(cells, sides, width):
    for axis, dim in sides:
        count = lax.axis_size(axis)
        ends = count - 1
        head = lax.slice_in_dim(cells, 0, width, axis=dim)
        tail = lax.slice_in_dim(cells, cells.shape[dim] - width, cells.shape[dim], axis=dim)
        cells = jnp.concatenate(
            [
                lax.ppermute(tail, axis, [(i, (i + 1) % count) for i in range(ends)]),
                cells,
                lax.ppermute(head, axis, [((i + 1) % count, i) for i in range(ends)]),
            ],
            axis=dim,
        )
    return cells


def tap_weights():
    raw_taps = [math.exp(-(offset - 4) * (offset - 4) / 4.5) for offset in range(9)]
    tap_total = sum(raw_taps)
    return [tap_value / tap_total for tap_value in raw_taps]


def smooth_axis(padded, axis):
    weights = tap_weights()
    length = padded.shape[axis] - 8
    summed = jnp.zeros(padded.shape[:axis] + (length,) + padded.shape[axis + 1 :], jnp.float32)
    for offset in range(9):
        summed = summed + weights[offset] * lax.slice_in_dim(
            padded, offset, offset + length, axis=axis
        )
    return summed


def pad_axis(field, axis):
    widths = [(0, 0)] * field.ndim
    widths[axis] = (4, 4)
    return jnp.pad(field, widths)


def lookup(indices, table):
    hits = indices[:, None] == jnp.arange(table.shape[0], dtype=jnp.int32)[None, :]
    return jnp.sum(jnp.where(hits, table[None, :], 0), axis=1)


def place(slots, values, total):
    hits = slots[None, :] == jnp.arange(total, dtype=jnp.int32)[:, None]
    return jnp.sum(jnp.where(hits, values[None, :] + 1, 0), axis=1) - 1


def same_channel(table, row_axis, column_axis):
    table = jnp.expand_dims(table, (row_axis, column_axis))
    shape = [1] * table.ndim
    shape[row_axis] = shape[column_axis] = GROUP
    return table & jnp.eye(GROUP, dtype=bool).reshape(shape)


def route_body(table_ref, cells_ref, out_ref):
    rows = cells_ref[...].reshape(-1, cells_ref.shape[-1])
    moved = jnp.dot(table_ref[...], rows, preferred_element_type=jnp.float32)
    out_ref[...] = moved.astype(out_ref.dtype).reshape(out_ref.shape)


def route(table, cells, spec, parts):
    groups = cells.shape[0] // GROUP if cells.ndim == 3 else cells.shape[1]
    rows = table.shape[0] // parts
    width = cells.shape[-1]
    return pl.pallas_call(
        route_body,
        grid=(groups,),
        in_specs=[pl.BlockSpec(table.shape, lambda g: (0, 0)), spec],
        out_specs=pl.BlockSpec((parts, 1, rows, width), lambda g: (0, g, 0, 0)),
        out_shape=jax.ShapeDtypeStruct((parts, groups, rows, width), cells.dtype),
        compiler_params=PARAMS,
    )(table, cells)


def pack(table, forward, parts):
    slots, stored = table.shape[1:]
    table = same_channel(table, 1, 3).astype(forward.dtype)
    table = table.reshape(parts * GROUP * slots, GROUP * stored)
    spec = pl.BlockSpec((GROUP,) + forward.shape[1:], lambda g: (g, 0, 0))
    return route(table, forward, spec, parts)


def reduce_body(count, *refs):
    tables, blocks, adjoint_ref, out_ref = refs[:count], refs[count : 2 * count], refs[-2], refs[-1]
    step = pl.program_id(0)
    local_tx, _, bricks, width = adjoint_ref.shape

    @pl.when(step == 0)
    def _():
        out_ref[...] = jnp.zeros_like(out_ref)

    summed = 0.0
    for table_ref, block_ref in zip(tables, blocks):
        rows = block_ref[...].reshape(-1, width)
        summed += jnp.dot(table_ref[...], rows, preferred_element_type=jnp.float32)
    summed = summed.reshape(GROUP, local_tx, bricks, width)
    for pair in range(GROUP // 2):
        total = 0.0
        for tx in range(local_tx):
            real = adjoint_ref[tx, 2 * pair].astype(jnp.float32)
            imag = adjoint_ref[tx, 2 * pair + 1].astype(jnp.float32)
            total += summed[2 * pair, tx] * real - summed[2 * pair + 1, tx] * imag
        vertical = lax.rem(step * (GROUP // 2) + pair, 3) == 2
        out_ref[0] += jnp.where(vertical, 0.0, total)
        out_ref[1] += jnp.where(vertical, total, 0.0)


def reduce(tables, blocks, adjoint):
    local_tx, channels, bricks, width = adjoint.shape
    flat = []
    for table in tables:
        last = table.ndim
        wide = same_channel(table, 0, last).astype(adjoint.dtype)
        flat.append(wide.reshape(GROUP * table.shape[0], -1))
    block_specs = [
        pl.BlockSpec((block.shape[0], 1) + block.shape[2:], lambda g: (0, g, 0, 0))
        for block in blocks
    ]
    return pl.pallas_call(
        functools.partial(reduce_body, len(flat)),
        grid=(channels // GROUP,),
        in_specs=[pl.BlockSpec(table.shape, lambda g: (0, 0)) for table in flat]
        + block_specs
        + [pl.BlockSpec((local_tx, GROUP, bricks, width), lambda g: (0, g, 0, 0))],
        out_specs=pl.BlockSpec((2, bricks, width), lambda g: (0, 0, 0)),
        out_shape=jax.ShapeDtypeStruct((2, bricks, width), jnp.float32),
        compiler_params=PARAMS,
    )(*flat, *blocks, adjoint)


def local(forward, item_tx, item_brick, tx_place, brick_place, adjoint):
    stored = forward.shape[0]
    src_count = lax.axis_size("src")
    vol_count = lax.axis_size("vol")
    devices = src_count * vol_count
    local_tx, local_bricks = adjoint.shape[:2]
    pairs = local_tx * local_bricks
    capacity = max(2, 2 * stored // devices)
    ranks = -(-max(capacity, DIRECT) // DIRECT) * DIRECT
    further = ranks - DIRECT
    both = ("src", "vol")

    tx_at = lookup(item_tx, tx_place)
    brick_at = lookup(item_brick, brick_place)
    plane = tx_at // local_tx
    column = brick_at // local_bricks
    owner = plane * vol_count + column
    pair = tx_at % local_tx * local_bricks + brick_at % local_bricks
    positions = jnp.arange(stored, dtype=jnp.int32)
    earlier = positions[:, None] > positions[None, :]
    rank = jnp.sum((owner[:, None] == owner[None, :]) & earlier, axis=1, dtype=jnp.int32)
    spilled = rank >= DIRECT
    before = earlier & spilled[None, :] & (plane[:, None] == plane[None, :])
    spill_rank = jnp.sum(before, axis=1, dtype=jnp.int32)
    late = spilled & (spill_rank >= SPILL)
    via = spilled & ~late

    channel_major = forward.transpose(1, 0, 2)
    adjoint_major = adjoint.transpose(0, 2, 1, 3)
    slot_ids = jnp.arange(DIRECT, dtype=jnp.int32)
    owner_ids = jnp.arange(devices, dtype=jnp.int32)
    pair_ids = jnp.arange(pairs, dtype=jnp.int32)

    listed = place(owner * ranks + rank, pair * 2 + late, devices * ranks)
    notes = [listed.reshape(src_count, vol_count, ranks)]
    if further:
        spill_slot = jnp.where(via, plane * SPILL + spill_rank, -1)
        codes = place(spill_slot, column * further + rank - DIRECT, src_count * SPILL)
        codes = codes.reshape(src_count, 1, SPILL)
        notes.append(jnp.broadcast_to(codes, (src_count, vol_count, SPILL)))
        any_late = jnp.max(late.astype(jnp.int32))
        notes.append(jnp.broadcast_to(any_late, (src_count, vol_count, 1)))
    notes = jnp.concatenate(notes, axis=2).reshape(devices, -1)
    notes = lax.all_to_all(notes, both, split_axis=0, concat_axis=0, tiled=True)
    notes = notes.reshape(src_count, vol_count, -1)
    listed = notes[..., :ranks]
    held = jnp.where((listed >= 0) & (listed % 2 == 0), listed // 2, -1)
    held_late = jnp.where((listed >= 0) & (listed % 2 == 1), listed // 2, -1)

    def send_direct(chosen, first):
        wanted = owner_ids[:, None] * DIRECT + slot_ids[None, :]
        slot = jnp.where(chosen, owner * DIRECT + rank - first, -1)
        packed = pack(wanted[:, :, None] == slot[None, None, :], channel_major, devices)
        return lax.all_to_all(packed, both, split_axis=0, concat_axis=0, tiled=True)

    def table_of(held_pairs):
        return held_pairs[None] == pair_ids.reshape((-1,) + (1,) * held_pairs.ndim)

    tables, blocks = [], []
    if further:
        wanted = jnp.arange(src_count * SPILL, dtype=jnp.int32).reshape(src_count, SPILL)
        packed = pack(wanted[:, :, None] == spill_slot[None, None, :], channel_major, src_count)
        spill = lax.all_to_all(packed, "src", split_axis=0, concat_axis=0, tiled=True)
    tables.append(table_of(held[..., :DIRECT].reshape(devices, DIRECT)))
    direct = send_direct(~spilled, 0)
    if further:
        codes = lax.dynamic_index_in_dim(notes, lax.axis_index("vol"), 1, keepdims=False)
        codes = codes[:, ranks : ranks + SPILL]
        wanted = jnp.arange(vol_count * further, dtype=jnp.int32).reshape(vol_count, 1, further, 1)
        table = wanted == codes[None, :, None, :]
        table = table[:, :, :, None, :] & jnp.eye(src_count, dtype=bool)[None, :, None, :, None]
        table = same_channel(table, 2, 5).astype(forward.dtype)
        table = table.reshape(vol_count * src_count * GROUP * further, -1)
        spec = pl.BlockSpec((src_count, 1) + spill.shape[2:], lambda g: (0, g, 0, 0))
        packed = route(table, spill, spec, vol_count)
        rest = lax.all_to_all(packed, "vol", split_axis=0, concat_axis=0, tiled=True)
        tables.append(table_of(held[..., DIRECT:].swapaxes(0, 1)))
        blocks.append(rest)
    blocks.insert(0, direct)
    raw = reduce(tables, blocks, adjoint_major)

    if further:
        def late_pass():
            total = jnp.zeros_like(raw)
            for first in range(DIRECT, ranks, DIRECT):
                chosen = late & (rank >= first) & (rank < first + DIRECT)
                kept = held_late[..., first : first + DIRECT].reshape(devices, DIRECT)
                total += reduce([table_of(kept)], [send_direct(chosen, first)], adjoint_major)
            return total

        raw = raw + lax.cond(jnp.max(notes[..., -1]) > 0, late_pass, lambda: jnp.zeros_like(raw))

    slab = (
        raw.reshape(2, NBY, NBZ, E, E, E)
        .transpose(0, 3, 1, 4, 2, 5)
        .reshape(2, E, NBY * E, NBZ * E)
    )
    summed = lax.psum(slab, "src")
    padded = with_halo(summed, (("vol", 1),), 4)
    field = smooth_axis(padded, 1)
    for axis in (2, 3):
        field = smooth_axis(pad_axis(field, axis), axis)
    return field


def solution(mesh):
    in_specs = (
        P(("src", "vol"), None, None),
        P(("src", "vol")),
        P(("src", "vol")),
        P(),
        P(),
        P("src", "vol", None, None),
    )
    out_specs = P(None, "vol", None, None)
    return jax.shard_map(local, mesh=mesh, in_specs=in_specs, out_specs=out_specs, check_vma=False)
```

time: 380 us -> 329 us (0.87)
  local copies, waits for them, and re-layouts: 80.8 us -> 13.8 us
  other arithmetic: 45.3 us -> 11.1 us
  Pallas kernels: 0 us -> 32.1 us
  starting transfers between devices: 20 us -> 29.3 us
  waiting for transfers between devices: 219 us -> 227 us
    pallas_call x0 -> x4, Pallas kernels: none -> 32.1 us  [the longest x3 21.3 us: route(): pl.pallas_call(route_body, grid=(groups,), in_specs=[pl.BlockSpec(table.s...]
    gather x2 -> x0, local copies, waits for them, and re-layouts: 23 us -> none  [local(): picked = flat_adjoint[jnp.maximum(arrived_pairs, 0)]]
    scatter x2 -> x0, local copies, waits for them, and re-layouts: 21.5 us -> none  [the longest x1 20.6 us: local(): jnp.zeros((slot_total, channels, cells), forward.dtype).at[slot_index]]
    sub x1 -> x2, other arithmetic: 14 us -> 0.01 us  [place(): return jnp.sum(jnp.where(hits, values[None, :] + 1, 0), axis=1) - 1]
    reshape x1, other arithmetic: 12.7 us -> 0.01 us  [local(): jnp.arange(vol_count * further, dtype=jnp.int32)]
    all_to_all x4 -> x0, local copies, waits for them, and re-layouts: 12.2 us -> none  [the longest x1 10.9 us: local(): lax.all_to_all(outgoing, ('src', 'vol'), split_axis=0, concat_axis=0, til...]
    all_to_all x2 -> x4, starting transfers between devices: 12.3 us -> 21.6 us  [the longest x1 6.44 us: local(): notes = lax.all_to_all(notes, both, split_axis=0, concat_axis=0, tiled=True)]
    convert_element_type x1 -> x5, other arithmetic: 12.7 us -> 3.97 us  [the longest x1 2.69 us: local(): table = same_channel(table, 2, 5).astype(forward.dtype)]
  transfers between devices with their start and end apart: 5 -> 7, of which waited for: 3 -> 5; matrix products, arithmetic and copies ran while one was open for 21% -> 3% of each run, Pallas kernels for 0% -> 5%
where the time goes in v1:
time: 329 us; the launch traced here: 328 us
  waiting for transfers between devices  227 us (69%)
  Pallas kernels  32.1 us (10%)
  starting transfers between devices  29.3 us (9%)
  between operations  14.4 us (4%)
  local copies, waits for them, and re-layouts  13.8 us (4%)
  other arithmetic  11.1 us (3%)
    all_to_all x1, waiting for transfers between devices, send_direct(): return lax.all_to_all(packed, both, split_axis=0, concat_axis=0, tiled=True)  103 us
    all_to_all x1, waiting for transfers between devices, local(): lax.all_to_all(packed, 'src', split_axis=0, concat_axis=0, tiled=True)  45.8 us
    all_to_all x1, waiting for transfers between devices, local(): lax.all_to_all(packed, 'vol', split_axis=0, concat_axis=0, tiled=True)  42.8 us
    psum x1, waiting for transfers between devices, local(): summed = lax.psum(slab, 'src')  32.2 us
    pallas_call x3, Pallas kernels, route(): pl.pallas_call(route_body, grid=(groups,), in_specs=[pl.BlockSpec(table.s...  21.3 us
    pallas_call x1, Pallas kernels, reduce(): pl.pallas_call(functools.partial(reduce_body, len(flat)), grid=(channels...  10.7 us
  transfers between devices with their start and end apart: 7, of which 5 were waited for; matrix products, arithmetic and copies ran while one was open for 3% of the time, Pallas kernels for 5%

profile of v1, /device:TPU:3, one launch (start us, length us, event | category | flops | bytes accessed | tf_op | source)
XLA Modules:
  0.0 327.7 jit_solution(9772008339680230968)
XLA Ops:
  11.0 6.4 %all-to-all-start.1 = ((s32[32,1,25]{2,1,0:T(1,128)}), s32[32,1,25]{2,1,0:T(1,128)S(1)}, u32[]{:S(2)}, u32[]{:S(2)}) async-start(s32[32,1,25]{2,1,0:T(1,128)} %bitcast.3), calls=%async_computation.1 | async-start | bytes 32768 | tf_op jit(solution)/shard_map/all_to_all | solution.py:196
  18.0 8.0 %shard_map.65 = bf16[4,9,64,512]{3,2,1,0:T(8,128)(2,1)} custom-call(bf16[256,512]{1,0:T(8,128)(2,1)S(1)} %bitcast.58, bf16[36,128,512]{2,1,0:T(8,128)(2,1)} %bitcast.59), custom_call_target="tpu_custom_call" | custom-call | tf_op jit(solution)/shard_map/pallas_call | solution.py:87
  27.5 4.3 %all-to-all-start.3 = ((bf16[4,9,64,512]{3,2,1,0:T(8,128)(2,1)}), bf16[4,9,64,512]{3,2,1,0:T(8,128)(2,1)S(1)}, u32[]{:S(2)}, u32[]{:S(2)}) async-start(bf16[4,9,64,512]{3,2,1,0:T(8,128)(2,1)} %shard_map.65), calls=%async_computation.3 | async-start | bytes 4718592 | tf_op jit(solution)/shard_map/all_to_all | solution.py:215
  32.1 2.7 and_convert_fusion.2
  34.8 4.6 %reshape.441.table_ref = bf16[512,256]{1,0:T(8,128)(2,1)S(1)} reshape(bf16[8,4,4,4,4,4,16]{6,5,4,3,2,1,0:T(4,128)(2,1)} %and_convert_fusion.2) | data formatting | bytes 524288 | tf_op jit(solution)/shard_map/convert_element_type | solution.py:224
  39.4 45.8 %all-to-all-done.3.cells_ref = bf16[4,9,64,512]{3,2,1,0:T(8,128)(2,1)S(1)} async-done(((bf16[4,9,64,512]{3,2,1,0:T(8,128)(2,1)}), bf16[4,9,64,512]{3,2,1,0:T(8,128)(2,1)S(1)}, u32[]{:S(2)}, u32[]{:S(2)}) %all-to-all-start.3) | async-done | bytes 2359328 | tf_op jit(solution)/shard_map/all_to_all | solution.py:215
  85.2 5.7 %shard_map.66 = bf16[8,9,64,512]{3,2,1,0:T(8,128)(2,1)} custom-call(bf16[512,256]{1,0:T(8,128)(2,1)S(1)} %reshape.441.table_ref, bf16[4,9,64,512]{3,2,1,0:T(8,128)(2,1)S(1)} %all-to-all-done.3.cells_ref), custom_call_target="tpu_custom_call" | custom-call | tf_op jit(solution)/shard_map/pallas_call | solution.py:87
  90.9 6.1 %all-to-all-start.4 = ((bf16[8,9,64,512]{3,2,1,0:T(8,128)(2,1)}), bf16[8,9,64,512]{3,2,1,0:T(8,128)(2,1)}, u32[]{:S(2)}, u32[]{:S(2)}) async-start(bf16[8,9,64,512]{3,2,1,0:T(8,128)(2,1)} %shard_map.66), calls=%async_computation.4 | async-start | bytes 9437184 | tf_op jit(solution)/shard_map/all_to_all | solution.py:228
  97.6 7.6 %shard_map.64 = bf16[32,9,16,512]{3,2,1,0:T(8,128)(2,1)S(1)} custom-call(bf16[512,512]{1,0:T(8,128)(2,1)S(1)} %bitcast.57, bf16[36,128,512]{2,1,0:T(8,128)(2,1)} %bitcast.61), custom_call_target="tpu_custom_call" | custom-call | tf_op jit(solution)/shard_map/pallas_call | solution.py:87
  105.2 2.2 copy-done
  107.5 42.8 %all-to-all-done.4.refs_3_ = bf16[8,9,64,512]{3,2,1,0:T(8,128)(2,1)} async-done(((bf16[8,9,64,512]{3,2,1,0:T(8,128)(2,1)}), bf16[8,9,64,512]{3,2,1,0:T(8,128)(2,1)}, u32[]{:S(2)}, u32[]{:S(2)}) %all-to-all-start.4) | async-done | bytes 4718624 | tf_op jit(solution)/shard_map/all_to_all | solution.py:228
  150.2 4.7 %all-to-all-start.2 = ((bf16[32,9,16,512]{3,2,1,0:T(8,128)(2,1)}), bf16[32,9,16,512]{3,2,1,0:T(8,128)(2,1)}, u32[]{:S(2)}, u32[]{:S(2)}) async-start(bf16[32,9,16,512]{3,2,1,0:T(8,128)(2,1)} %copy-done), calls=%async_computation.2 | async-start | bytes 9437184 | tf_op jit(solution)/shard_map/all_to_all | solution.py:206
  156.7 102.6 %all-to-all-done.2.refs_2_ = bf16[32,9,16,512]{3,2,1,0:T(8,128)(2,1)} async-done(((bf16[32,9,16,512]{3,2,1,0:T(8,128)(2,1)}), bf16[32,9,16,512]{3,2,1,0:T(8,128)(2,1)}, u32[]{:S(2)}, u32[]{:S(2)}) %all-to-all-start.2) | async-done | bytes 4718624 | tf_op jit(solution)/shard_map/all_to_all | solution.py:206
  259.3 10.7 %shard_map.67 = f32[2,32,512]{2,1,0:T(8,128)S(1)} custom-call(bf16[512,512]{1,0:T(8,128)(2,1)S(1)} %copy.63.refs_0_, bf16[512,512]{1,0:T(8,128)(2,1)S(1)} %copy.64.refs_1_, bf16[32,9,16,512]{3,2,1,0:T(8,128)(2,1)} %all-to-all-done.2.refs_2_, bf16[8,9,64,512]{3,2,1,0:T(8,128)(2,1)} %all-to-all-done.4.refs_3_, bf16[4,36,32,512]{3,2,1,0:T(8,128)(2,1)} %bitcast.63), custom_call_target="tpu_custom_call" | custom-call | tf_op jit(solution)/shard_map/pallas_call | solution.py:141
  270.9 0.9 copy.71
  271.8 1.6 reshape.435
  273.4 32.2 %all-reduce.4.cloned.1.call-done = f32[2,8,16,128]{3,2,1,0:T(8,128)} async-done(((f32[2,8,16,128]{3,2,1,0:T(8,128)}), f32[2,8,16,128]{3,2,1,0:T(8,128)}) %all-reduce.4.cloned.1.call-update) | async-done | bytes 131088 | tf_op jit(solution)/shard_map/psum | solution.py:250
  305.6 0.9 fusion.48
  306.5 5.7 %collective-permute-start = (f32[2,4,16,128]{3,2,1,0:T(8,128)S(1)}, f32[2,4,16,128]{3,2,1,0:T(8,128)S(1)}, u32[]{:S(2)}, u32[]{:S(2)}) collective-permute-start(f32[2,4,16,128]{3,2,1,0:T(8,128)S(1)} %get-tuple-element.189), channel_id=1, source_target_pairs={{0,1},{1,2},{2,3},{3,4},{4,5},{5,6},{6,7},{8,9},{9,10},{10,11},{11... | collective-permute-start | bytes 196616 | tf_op jit(solution)/shard_map/ppermute | solution.py:28
  312.2 1.9 collective-permute-start.1
  314.1 0.9 constant_dynamic-update-slice_fusion
  315.1 3.6 %collective-permute-done.1 = f32[2,4,16,128]{3,2,1,0:T(8,128)S(1)} collective-permute-done((f32[2,4,16,128]{3,2,1,0:T(8,128)S(1)}, f32[2,4,16,128]{3,2,1,0:T(8,128)S(1)}, u32[]{:S(2)}, u32[]{:S(2)}) %collective-permute-start.1) | collective-permute-done | bytes 65568 | tf_op jit(solution)/shard_map/ppermute | solution.py:30
  318.7 1.0 fusion.33
  319.8 1.0 fusion.25
  (67 shorter events, 9.3 us)
Async XLA Ops:
  11.0 14.9 %all-to-all-start.1 = ((s32[32,1,25]{2,1,0:T(1,128)}), s32[32,1,25]{2,1,0:T(1,128)S(1)}, u32[]{:S(2)}, u32[]{:S(2)}) async-start(s32[32,1,25]{2,1,0:T(1,128)} %bitcast.3), calls=%async_computation.1 | async-start | bytes 32768 | tf_op jit(solution)/shard_map/all_to_all | solution.py:196
  27.5 57.7 %all-to-all-start.3 = ((bf16[4,9,64,512]{3,2,1,0:T(8,128)(2,1)}), bf16[4,9,64,512]{3,2,1,0:T(8,128)(2,1)S(1)}, u32[]{:S(2)}, u32[]{:S(2)}) async-start(bf16[4,9,64,512]{3,2,1,0:T(8,128)(2,1)} %shard_map.65), calls=%async_computation.3 | async-start | bytes 4718592 | tf_op jit(solution)/shard_map/all_to_all | solution.py:215
  90.9 59.3 %all-to-all-start.4 = ((bf16[8,9,64,512]{3,2,1,0:T(8,128)(2,1)}), bf16[8,9,64,512]{3,2,1,0:T(8,128)(2,1)}, u32[]{:S(2)}, u32[]{:S(2)}) async-start(bf16[8,9,64,512]{3,2,1,0:T(8,128)(2,1)} %shard_map.66), calls=%async_computation.4 | async-start | bytes 9437184 | tf_op jit(solution)/shard_map/all_to_all | solution.py:228
  105.2 2.2 copy-start
  150.2 109.1 %all-to-all-start.2 = ((bf16[32,9,16,512]{3,2,1,0:T(8,128)(2,1)}), bf16[32,9,16,512]{3,2,1,0:T(8,128)(2,1)}, u32[]{:S(2)}, u32[]{:S(2)}) async-start(bf16[32,9,16,512]{3,2,1,0:T(8,128)(2,1)} %copy-done), calls=%async_computation.2 | async-start | bytes 9437184 | tf_op jit(solution)/shard_map/all_to_all | solution.py:206
  155.0 150.6 %all-reduce.4.cloned.1.call-start = ((), (), s32[]{:S(2)}) async-start(), calls=%async_computation.5 | async-start | bytes 262144 | tf_op jit(solution)/shard_map/psum | solution.py:250
  306.5 7.7 %collective-permute-start = (f32[2,4,16,128]{3,2,1,0:T(8,128)S(1)}, f32[2,4,16,128]{3,2,1,0:T(8,128)S(1)}, u32[]{:S(2)}, u32[]{:S(2)}) collective-permute-start(f32[2,4,16,128]{3,2,1,0:T(8,128)S(1)} %get-tuple-element.189), channel_id=1, source_target_pairs={{0,1},{1,2},{2,3},{3,4},{4,5},{5,6},{6,7},{8,9},{9,10},{10,11},{11... | collective-permute-start | bytes 196616 | tf_op jit(solution)/shard_map/ppermute | solution.py:28
  312.2 6.5 %collective-permute-start.1 = (f32[2,4,16,128]{3,2,1,0:T(8,128)S(1)}, f32[2,4,16,128]{3,2,1,0:T(8,128)S(1)}, u32[]{:S(2)}, u32[]{:S(2)}) collective-permute-start(f32[2,4,16,128]{3,2,1,0:T(8,128)S(1)} %get-tuple-element.190), channel_id=1, source_target_pairs={{1,0},{2,1},{3,2},{4,3},{5,4},{6,5},{7,6},{9,8},{10,9},{11,10},{12... | collective-permute-start | bytes 196616 | tf_op jit(solution)/shard_map/ppermute | solution.py:30
Sparse Core Ops, SparseCore 0:
  273.5 32.0 all-reduce.3

commit v2 on v1

--- a/solution.py
+++ b/solution.py
@@ -102,19 +102,236 @@
     return route(table, forward, spec, parts)
 
 
-def reduce_body(count, *refs):
-    tables, blocks, adjoint_ref, out_ref = refs[:count], refs[count : 2 * count], refs[-2], refs[-1]
+def row_ids(shape, slots):
+    row = lax.broadcasted_iota(jnp.int32, shape, 0)
+    part, inner = row // (GROUP * slots), row % (GROUP * slots)
+    return part * slots + inner % slots, inner // slots
+
+
+def pick_table(wanted, row_channel, per_channel):
+    column = lax.broadcasted_iota(jnp.int32, row_channel.shape, 1) // per_channel
+    return jnp.where(wanted & (row_channel == column), 1.0, 0.0).astype(jnp.bfloat16)
+
+
+def exchange_body(src_count, vol_count, further, *refs):
+    if further:
+        (slots_ref, codes_ref, notes_ref, cells_ref, direct_in, notes_in, rest_in) = refs[:7]
+        (direct_out, sends, receives, own, spill_out, spill_in, codes_in, rest_out) = refs[7:15]
+        (spill_sends, spill_receives, rest_sends, rest_receives) = refs[15:]
+    else:
+        (slots_ref, notes_ref, cells_ref, direct_in, notes_in) = refs[:5]
+        (direct_out, sends, receives, own) = refs[5:]
+    my_src, my_vol = lax.axis_index("src"), lax.axis_index("vol")
+    devices = src_count * vol_count
+    me = my_src * vol_count + my_vol
+    channels, stored, width = cells_ref.shape
+    groups = channels // GROUP
+    mesh_ids = pl.DeviceIdType.MESH
+
+    barrier = pltpu.get_barrier_semaphore()
+
+    def greet(step, carry):
+        peer = lax.rem(me + step, devices)
+        pl.semaphore_signal(
+            barrier,
+            inc=1,
+            device_id=(peer // vol_count, lax.rem(peer, vol_count)),
+            device_id_type=mesh_ids,
+        )
+        return carry
+
+    lax.fori_loop(1, devices, greet, 0)
+
+    def pack_into(out, parts, slots, row):
+        shape = (parts * GROUP * slots, GROUP * stored)
+        number, channel = row_ids(shape, slots)
+        holders = slots_ref[row : row + 1, :]
+        holders = jnp.concatenate([holders] * GROUP, axis=1)
+        table = pick_table(number == holders, channel, stored)
+
+        def pack_group(group, carry):
+            cells = cells_ref[pl.ds(group * GROUP, GROUP)].reshape(GROUP * stored, width)
+            moved = jnp.dot(table, cells, preferred_element_type=jnp.float32)
+            out[:, group] = moved.astype(jnp.bfloat16).reshape(parts, GROUP * slots, width)
+            return carry
+
+        lax.fori_loop(0, groups, pack_group, 0)
+
+    def spill_copies(hop):
+        plane = lax.rem(my_src + hop, src_count)
+        return [
+            pltpu.make_async_remote_copy(
+                src_ref=source.at[plane],
+                dst_ref=target.at[my_src],
+                send_sem=spill_sends.at[kind, hop],
+                recv_sem=spill_receives.at[kind, hop],
+                device_id=(plane, my_vol),
+                device_id_type=mesh_ids,
+            )
+            for kind, (source, target) in enumerate(
+                ((codes_ref, codes_in), (spill_out, spill_in))
+            )
+        ]
+
+    def direct_copies(hop, turn):
+        plane = lax.rem(my_src + hop, src_count)
+        column = lax.rem(my_vol + turn, vol_count)
+        peer = plane * vol_count + column
+        return [
+            pltpu.make_async_remote_copy(
+                src_ref=source.at[peer],
+                dst_ref=target.at[me],
+                send_sem=sends.at[kind, hop * vol_count + turn],
+                recv_sem=receives.at[kind, hop * vol_count + turn],
+                device_id=(plane, column),
+                device_id_type=mesh_ids,
+            )
+            for kind, (source, target) in enumerate(
+                ((notes_ref, notes_in), (direct_out, direct_in))
+            )
+        ]
+
+    def rest_copy(origin, hop, turn):
+        column = lax.rem(my_vol + turn, vol_count)
+        return pltpu.make_async_remote_copy(
+            src_ref=rest_out.at[origin, column],
+            dst_ref=rest_in.at[origin * vol_count + my_vol],
+            send_sem=rest_sends.at[hop, turn],
+            recv_sem=rest_receives.at[hop, turn],
+            device_id=(my_src, column),
+            device_id_type=mesh_ids,
+        )
+
+    def each_turn(hop, act):
+        def body(turn, carry):
+            act(turn)
+            return carry
+
+        lax.fori_loop(1 if hop == 0 else 0, vol_count, body, 0)
+
+    hops = sorted(range(src_count), key=lambda hop: (hop == 0, abs(2 * hop - src_count), hop))
+    if further:
+        pack_into(spill_out, src_count, SPILL, 1)
+    pl.semaphore_wait(barrier, devices - 1)
+    if further:
+        for hop in hops:
+            if hop:
+                for copy in spill_copies(hop):
+                    copy.start()
+    pack_into(direct_out, devices, DIRECT, 0)
+    for hop in hops:
+
+        def begin(turn):
+            for copy in direct_copies(hop, turn):
+                copy.start()
+
+        each_turn(hop, begin)
+    kept = [
+        pltpu.make_async_copy(direct_out.at[me], direct_in.at[me], own.at[0]),
+        pltpu.make_async_copy(notes_ref.at[me], notes_in.at[me], own.at[1]),
+    ]
+    if further:
+        for hop in sorted(range(src_count), key=lambda hop: (min(hop, src_count - hop), hop)):
+            origin = lax.rem(my_src + src_count - hop, src_count)
+            if hop:
+                for copy in spill_copies(hop):
+                    copy.wait_recv()
+            codes, spill = (codes_in, spill_in) if hop else (codes_ref, spill_out)
+            code = codes[origin].astype(jnp.float32)[0:1, : GROUP * SPILL].astype(jnp.int32)
+            number, channel = row_ids((vol_count * GROUP * further, GROUP * SPILL), further)
+            table = pick_table(number == code, channel, SPILL)
+
+            def repack(group, carry):
+                moved = jnp.dot(table, spill[origin, group], preferred_element_type=jnp.float32)
+                moved = moved.astype(jnp.bfloat16)
+                rest_out[origin, :, group] = moved.reshape(vol_count, GROUP * further, width)
+                return carry
+
+            lax.fori_loop(0, groups, repack, 0)
+            each_turn(0, lambda turn: rest_copy(origin, hop, turn).start())
+            kept.append(
+                pltpu.make_async_copy(
+                    rest_out.at[origin, my_vol],
+                    rest_in.at[origin * vol_count + my_vol],
+                    own.at[2 + hop],
+                )
+            )
+    for copy in kept:
+        copy.start()
+    for copy in kept:
+        copy.wait()
+    if further:
+        for hop in range(1, src_count):
+            for copy in spill_copies(hop):
+                copy.wait_send()
+        for hop in range(src_count):
+            origin = lax.rem(my_src + src_count - hop, src_count)
+            each_turn(0, lambda turn: rest_copy(origin, hop, turn).wait())
+    for hop in hops:
+
+        def finish(turn):
+            for copy in direct_copies(hop, turn):
+                copy.wait()
+
+        each_turn(hop, finish)
+
+
+def exchange(slots, codes, notes, cells, src_count, vol_count, further):
+    channels, _, width = cells.shape
+    groups = channels // GROUP
+    devices = src_count * vol_count
+    kind = cells.dtype
+    chunk = (groups, GROUP * DIRECT, width)
+    inputs = [slots] + ([codes] if further else []) + [notes, cells]
+    outputs = [(devices,) + chunk, notes.shape] + ([(devices,) + chunk] if further else [])
+    dma = pltpu.SemaphoreType.DMA
+    scratch = [
+        pltpu.VMEM((devices,) + chunk, kind),
+        dma((2, devices)),
+        dma((2, devices)),
+        dma((2 + src_count,)),
+    ]
+    if further:
+        spill = pltpu.VMEM((src_count, groups, GROUP * SPILL, width), kind)
+        scratch += [spill, spill, pltpu.VMEM(codes.shape, codes.dtype)]
+        scratch += [pltpu.VMEM((src_count, vol_count) + chunk, kind)]
+        scratch += [dma((2, src_count))] * 2 + [dma((src_count, vol_count))] * 2
+    return pl.pallas_call(
+        functools.partial(exchange_body, src_count, vol_count, further),
+        in_specs=[pl.BlockSpec(memory_space=pltpu.VMEM)] * len(inputs),
+        out_specs=[pl.BlockSpec(memory_space=pl.ANY)] * len(outputs),
+        out_shape=[jax.ShapeDtypeStruct(shape, kind) for shape in outputs],
+        scratch_shapes=scratch,
+        compiler_params=pltpu.CompilerParams(
+            collective_id=0, has_side_effects=True, vmem_limit_bytes=56 * 1024 * 1024
+        ),
+    )(*inputs)
+
+
+def reduce_body(firsts, notes_ref, *refs):
+    count = len(firsts)
+    blocks, (adjoint_ref, out_ref, tables) = refs[:count], refs[count:]
     step = pl.program_id(0)
     local_tx, _, bricks, width = adjoint_ref.shape
+    pairs = local_tx * bricks
 
     @pl.when(step == 0)
     def _():
         out_ref[...] = jnp.zeros_like(out_ref)
+        notes = notes_ref[...].astype(jnp.float32)
+        for at, first in enumerate(firsts):
+            rows = notes[:, first : first + DIRECT]
+            rows = jnp.concatenate([rows] * GROUP, axis=1).reshape(-1, pairs)
+            rows = rows.T
+            channel = lax.broadcasted_iota(jnp.int32, rows.shape, 1) // DIRECT % GROUP
+            for group in range(GROUP):
+                kept = jnp.where(channel == group, rows, 0.0).astype(tables.dtype)
+                tables[at, group * pairs : (group + 1) * pairs] = kept
 
     summed = 0.0
-    for table_ref, block_ref in zip(tables, blocks):
+    for at, block_ref in enumerate(blocks):
         rows = block_ref[...].reshape(-1, width)
-        summed += jnp.dot(table_ref[...], rows, preferred_element_type=jnp.float32)
+        summed += jnp.dot(tables[at], rows, preferred_element_type=jnp.float32)
     summed = summed.reshape(GROUP, local_tx, bricks, width)
     for pair in range(GROUP // 2):
         total = 0.0
@@ -127,27 +344,22 @@
         out_ref[1] += jnp.where(vertical, total, 0.0)
 
 
-def reduce(tables, blocks, adjoint):
+def reduce(notes, firsts, blocks, adjoint):
     local_tx, channels, bricks, width = adjoint.shape
-    flat = []
-    for table in tables:
-        last = table.ndim
-        wide = same_channel(table, 0, last).astype(adjoint.dtype)
-        flat.append(wide.reshape(GROUP * table.shape[0], -1))
-    block_specs = [
-        pl.BlockSpec((block.shape[0], 1) + block.shape[2:], lambda g: (0, g, 0, 0))
-        for block in blocks
-    ]
+    sources = notes.shape[0]
+    block = pl.BlockSpec((sources, 1) + blocks[0].shape[2:], lambda g: (0, g, 0, 0))
+    table = (len(firsts), GROUP * local_tx * bricks, sources * GROUP * DIRECT)
     return pl.pallas_call(
-        functools.partial(reduce_body, len(flat)),
+        functools.partial(reduce_body, firsts),
         grid=(channels // GROUP,),
-        in_specs=[pl.BlockSpec(table.shape, lambda g: (0, 0)) for table in flat]
-        + block_specs
+        in_specs=[pl.BlockSpec(notes.shape, lambda g: (0, 0, 0))]
+        + [block] * len(blocks)
         + [pl.BlockSpec((local_tx, GROUP, bricks, width), lambda g: (0, g, 0, 0))],
         out_specs=pl.BlockSpec((2, bricks, width), lambda g: (0, 0, 0)),
         out_shape=jax.ShapeDtypeStruct((2, bricks, width), jnp.float32),
+        scratch_shapes=[pltpu.VMEM(table, jnp.bfloat16)],
         compiler_params=PARAMS,
-    )(*flat, *blocks, adjoint)
+    )(notes, *blocks, adjoint)
 
 
 def local(forward, item_tx, item_brick, tx_place, brick_place, adjoint):
@@ -158,9 +370,11 @@
     local_tx, local_bricks = adjoint.shape[:2]
     pairs = local_tx * local_bricks
     capacity = max(2, 2 * stored // devices)
-    ranks = -(-max(capacity, DIRECT) // DIRECT) * DIRECT
-    further = ranks - DIRECT
+    further = DIRECT if capacity > DIRECT else 0
+    ranks = DIRECT + further
+    assert capacity <= 2 * DIRECT
     both = ("src", "vol")
+    kind = forward.dtype
 
     tx_at = lookup(item_tx, tx_place)
     brick_at = lookup(item_brick, brick_place)
@@ -175,72 +389,37 @@
     before = earlier & spilled[None, :] & (plane[:, None] == plane[None, :])
     spill_rank = jnp.sum(before, axis=1, dtype=jnp.int32)
     late = spilled & (spill_rank >= SPILL)
-    via = spilled & ~late
 
     channel_major = forward.transpose(1, 0, 2)
     adjoint_major = adjoint.transpose(0, 2, 1, 3)
-    slot_ids = jnp.arange(DIRECT, dtype=jnp.int32)
-    owner_ids = jnp.arange(devices, dtype=jnp.int32)
-    pair_ids = jnp.arange(pairs, dtype=jnp.int32)
-
-    listed = place(owner * ranks + rank, pair * 2 + late, devices * ranks)
-    notes = [listed.reshape(src_count, vol_count, ranks)]
-    if further:
-        spill_slot = jnp.where(via, plane * SPILL + spill_rank, -1)
+
+    note_rank = jnp.where(late, rank + DIRECT, rank)
+    listed = place(owner * 16 + note_rank, pair, devices * 16).reshape(devices, 16)
+    notes = listed[:, :, None] == jnp.arange(pairs, dtype=jnp.int32)[None, None, :]
+    flag_row = jnp.arange(16, dtype=jnp.int32)[None, :, None] == 15
+    notes = jnp.where(flag_row, jnp.any(late), notes).astype(kind)
+    direct_slot = jnp.where(spilled, -1, owner * DIRECT + rank)
+    spill_slot = jnp.where(spilled & ~late, plane * SPILL + spill_rank, -1)
+    slots = jnp.zeros((8, stored), jnp.int32).at[0].set(direct_slot).at[1].set(spill_slot)
+    codes = None
+    if further:
         codes = place(spill_slot, column * further + rank - DIRECT, src_count * SPILL)
-        codes = codes.reshape(src_count, 1, SPILL)
-        notes.append(jnp.broadcast_to(codes, (src_count, vol_count, SPILL)))
-        any_late = jnp.max(late.astype(jnp.int32))
-        notes.append(jnp.broadcast_to(any_late, (src_count, vol_count, 1)))
-    notes = jnp.concatenate(notes, axis=2).reshape(devices, -1)
-    notes = lax.all_to_all(notes, both, split_axis=0, concat_axis=0, tiled=True)
-    notes = notes.reshape(src_count, vol_count, -1)
-    listed = notes[..., :ranks]
-    held = jnp.where((listed >= 0) & (listed % 2 == 0), listed // 2, -1)
-    held_late = jnp.where((listed >= 0) & (listed % 2 == 1), listed // 2, -1)
-
-    def send_direct(chosen, first):
-        wanted = owner_ids[:, None] * DIRECT + slot_ids[None, :]
-        slot = jnp.where(chosen, owner * DIRECT + rank - first, -1)
-        packed = pack(wanted[:, :, None] == slot[None, None, :], channel_major, devices)
-        return lax.all_to_all(packed, both, split_axis=0, concat_axis=0, tiled=True)
-
-    def table_of(held_pairs):
-        return held_pairs[None] == pair_ids.reshape((-1,) + (1,) * held_pairs.ndim)
-
-    tables, blocks = [], []
-    if further:
-        wanted = jnp.arange(src_count * SPILL, dtype=jnp.int32).reshape(src_count, SPILL)
-        packed = pack(wanted[:, :, None] == spill_slot[None, None, :], channel_major, src_count)
-        spill = lax.all_to_all(packed, "src", split_axis=0, concat_axis=0, tiled=True)
-    tables.append(table_of(held[..., :DIRECT].reshape(devices, DIRECT)))
-    direct = send_direct(~spilled, 0)
-    if further:
-        codes = lax.dynamic_index_in_dim(notes, lax.axis_index("vol"), 1, keepdims=False)
-        codes = codes[:, ranks : ranks + SPILL]
-        wanted = jnp.arange(vol_count * further, dtype=jnp.int32).reshape(vol_count, 1, further, 1)
-        table = wanted == codes[None, :, None, :]
-        table = table[:, :, :, None, :] & jnp.eye(src_count, dtype=bool)[None, :, None, :, None]
-        table = same_channel(table, 2, 5).astype(forward.dtype)
-        table = table.reshape(vol_count * src_count * GROUP * further, -1)
-        spec = pl.BlockSpec((src_count, 1) + spill.shape[2:], lambda g: (0, g, 0, 0))
-        packed = route(table, spill, spec, vol_count)
-        rest = lax.all_to_all(packed, "vol", split_axis=0, concat_axis=0, tiled=True)
-        tables.append(table_of(held[..., DIRECT:].swapaxes(0, 1)))
-        blocks.append(rest)
-    blocks.insert(0, direct)
-    raw = reduce(tables, blocks, adjoint_major)
-
-    if further:
+        codes = jnp.tile(codes.reshape(src_count, 1, SPILL), (1, 16, 128 // SPILL)).astype(kind)
+    moved = exchange(slots, codes, notes, channel_major, src_count, vol_count, further)
+    notes = moved[1]
+    firsts = (0, DIRECT) if further else (0,)
+    raw = reduce(notes, firsts, [moved[0]] + list(moved[2:]), adjoint_major)
+
+    if further:
+
         def late_pass():
-            total = jnp.zeros_like(raw)
-            for first in range(DIRECT, ranks, DIRECT):
-                chosen = late & (rank >= first) & (rank < first + DIRECT)
-                kept = held_late[..., first : first + DIRECT].reshape(devices, DIRECT)
-                total += reduce([table_of(kept)], [send_direct(chosen, first)], adjoint_major)
-            return total
-
-        raw = raw + lax.cond(jnp.max(notes[..., -1]) > 0, late_pass, lambda: jnp.zeros_like(raw))
+            wanted = jnp.arange(devices * DIRECT, dtype=jnp.int32).reshape(devices, DIRECT)
+            slot = jnp.where(late, owner * DIRECT + rank - DIRECT, -1)
+            packed = pack(wanted[:, :, None] == slot[None, None, :], channel_major, devices)
+            bricks = lax.all_to_all(packed, both, split_axis=0, concat_axis=0, tiled=True)
+            return raw + reduce(notes, (2 * DIRECT,), [bricks], adjoint_major)
+
+        raw = lax.cond(jnp.max(notes[:, 15, 0]) > 0, late_pass, lambda: raw)
 
     slab = (
         raw.reshape(2, NBY, NBZ, E, E, E)

time: 329 us -> 250 us (0.76)
  waiting for transfers between devices: 227 us -> 58.9 us
  Pallas kernels: 32.1 us -> 153 us
  starting transfers between devices: 29.3 us -> 7.64 us
  local copies, waits for them, and re-layouts: 13.8 us -> 8.31 us
  other arithmetic: 11.1 us -> 7.28 us
    all_to_all x4 -> x0, waiting for transfers between devices: 191 us -> none  [the longest x1 103 us: send_direct(): return lax.all_to_all(packed, both, split_axis=0, concat_axis=0, tiled=True)]
    pallas_call x4 -> x2, Pallas kernels: 32.1 us -> 153 us  [the longest x1 142 us: exchange(): pl.pallas_call(functools.partial(exchange_body, src_count, vol_count, fur...]
    psum x1, waiting for transfers between devices: 32.2 us -> 55.3 us  [local(): summed = lax.psum(slab, 'src')]
    all_to_all x4 -> x0, starting transfers between devices: 21.6 us -> none  [the longest x1 6.44 us: local(): notes = lax.all_to_all(notes, both, split_axis=0, concat_axis=0, tiled=True)]
    convert_element_type x3 -> x2, local copies, waits for them, and re-layouts: 5.02 us -> 0.17 us  [local(): jnp.tile(codes.reshape(src_count, 1, SPILL), (1, 16, 128 // SPILL))]
  transfers between devices with their start and end apart: 7 -> 3, of which waited for: 5 -> 2; matrix products, arithmetic and copies ran while one was open for 3% -> 0% of each run, Pallas kernels for 5% -> 0%
where the time goes in v2:
time: 250 us; the launch traced here: 249 us
  Pallas kernels  153 us (61%)
  waiting for transfers between devices  58.9 us (24%)
  between operations  14.2 us (6%)
  local copies, waits for them, and re-layouts  8.31 us (3%)
  starting transfers between devices  7.64 us (3%)
  other arithmetic  7.28 us (3%)
    pallas_call x1, Pallas kernels, exchange(): pl.pallas_call(functools.partial(exchange_body, src_count, vol_count, fur...  142 us
    psum x1, waiting for transfers between devices, local(): summed = lax.psum(slab, 'src')  55.3 us
    pallas_call x1, Pallas kernels, reduce(): pl.pallas_call(functools.partial(reduce_body, firsts), grid=(channels //...  10.3 us
    ppermute x1, starting transfers between devices, with_halo(): lax.ppermute(tail, axis, [(i, (i + 1) % count) for i in range(ends)])  5.72 us
  transfers between devices with their start and end apart: 3, of which 2 were waited for; matrix products, arithmetic and copies ran while one was open for 0% of the time, Pallas kernels for 0%

profile of v2, /device:TPU:3, one launch (start us, length us, event | category | flops | bytes accessed | tf_op | source)
XLA Modules:
  0.0 249.0 jit_solution(10089586062783088852)
XLA Ops:
  6.5 0.8 select_reduce_fusion.3
  7.3 0.8 select_reduce_fusion.1
  8.2 0.2 convert_reduce_fusion.1
  8.4 0.2 convert_reduce_fusion
  8.6 0.7 compare_and_fusion
  9.5 0.2 select_reduce_fusion
  9.9 1.5 fusion.1.refs_2_
  11.4 0.6 tile.9.refs_1_
  12.0 142.4 %shard_map.64 = (bf16[32,9,16,512]{3,2,1,0:T(8,128)(2,1)}, bf16[32,16,128]{2,1,0:T(8,128)(2,1)S(1)}, bf16[32,9,16,512]{3,2,1,0:T(8,128)(2,1)}) custom-call(s32[8,128]{1,0:T(8,128)} %copy-done.1, bf16[4,16,128]{2,1,0:T(8,128)(2,1)} %tile.9.refs_1_, bf16[32,16,128]{2,1,0:T(8,128)(2,1)} %fusion.1.refs_2_, bf16[36,128,512]{2,1,0:T(8,128)(2,1)} %bitcast.50), custom_call_target="tpu_custom_call" | custom-call | tf_op jit(solution)/shard_map/pallas_call | solution.py:299
  154.4 0.6 slice_reduce_fusion
  155.7 2.3 copy-done
  158.0 10.3 %shard_map.65 = f32[2,32,512]{2,1,0:T(8,128)S(1)} custom-call(bf16[32,16,128]{2,1,0:T(8,128)(2,1)S(1)} %get-tuple-element.57.notes_ref, bf16[32,9,16,512]{3,2,1,0:T(8,128)(2,1)S(1)} %copy-done, bf16[32,9,16,512]{3,2,1,0:T(8,128)(2,1)} %get-tuple-element.59.refs_1_, bf16[4,36,32,512]{3,2,1,0:T(8,128)(2,1)} %bitcast.46), custom_call_target="tpu_custom_call" | custom-call | tf_op jit(solution)/shard_map/pallas_call | solution.py:352
  168.3 0.2 copy.10
  168.5 0.6 reshape.361
  169.1 0.9 copy.11
  170.0 1.6 reshape.362
  171.6 55.3 %all-reduce.5.cloned.1.call-done = f32[2,8,16,128]{3,2,1,0:T(8,128)} async-done(((f32[2,8,16,128]{3,2,1,0:T(8,128)}), f32[2,8,16,128]{3,2,1,0:T(8,128)}) %all-reduce.5.cloned.1.call-update) | async-done | bytes 131088 | tf_op jit(solution)/shard_map/psum | solution.py:429
  226.9 0.9 fusion.50
  227.8 5.7 %collective-permute-start = (f32[2,4,16,128]{3,2,1,0:T(8,128)S(1)}, f32[2,4,16,128]{3,2,1,0:T(8,128)S(1)}, u32[]{:S(2)}, u32[]{:S(2)}) collective-permute-start(f32[2,4,16,128]{3,2,1,0:T(8,128)S(1)} %get-tuple-element.65), channel_id=1, source_target_pairs={{0,1},{1,2},{2,3},{3,4},{4,5},{5,6},{6,7},{8,9},{9,10},{10,11},{11... | collective-permute-start | bytes 196616 | tf_op jit(solution)/shard_map/ppermute | solution.py:28
  233.6 1.9 collective-permute-start.1
  235.5 0.9 constant_dynamic-update-slice_fusion
  236.4 3.6 %collective-permute-done.1 = f32[2,4,16,128]{3,2,1,0:T(8,128)S(1)} collective-permute-done((f32[2,4,16,128]{3,2,1,0:T(8,128)S(1)}, f32[2,4,16,128]{3,2,1,0:T(8,128)S(1)}, u32[]{:S(2)}, u32[]{:S(2)}) %collective-permute-start.1) | collective-permute-done | bytes 65568 | tf_op jit(solution)/shard_map/ppermute | solution.py:30
  240.0 1.0 fusion.34
  241.2 1.0 fusion.26
  (24 shorter events, 0.7 us)
Async XLA Ops:
  6.5 220.4 %all-reduce.5.cloned.1.call-start = ((), (), s32[]{:S(2)}) async-start(), calls=%async_computation.1 | async-start | bytes 262144 | tf_op jit(solution)/shard_map/psum | solution.py:429
  9.9 2.1 copy-start.1
  155.7 2.3 copy-start
  227.8 7.7 %collective-permute-start = (f32[2,4,16,128]{3,2,1,0:T(8,128)S(1)}, f32[2,4,16,128]{3,2,1,0:T(8,128)S(1)}, u32[]{:S(2)}, u32[]{:S(2)}) collective-permute-start(f32[2,4,16,128]{3,2,1,0:T(8,128)S(1)} %get-tuple-element.65), channel_id=1, source_target_pairs={{0,1},{1,2},{2,3},{3,4},{4,5},{5,6},{6,7},{8,9},{9,10},{10,11},{11... | collective-permute-start | bytes 196616 | tf_op jit(solution)/shard_map/ppermute | solution.py:28
  233.6 6.5 %collective-permute-start.1 = (f32[2,4,16,128]{3,2,1,0:T(8,128)S(1)}, f32[2,4,16,128]{3,2,1,0:T(8,128)S(1)}, u32[]{:S(2)}, u32[]{:S(2)}) collective-permute-start(f32[2,4,16,128]{3,2,1,0:T(8,128)S(1)} %get-tuple-element.66), channel_id=1, source_target_pairs={{1,0},{2,1},{3,2},{4,3},{5,4},{6,5},{7,6},{9,8},{10,9},{11,10},{12... | collective-permute-start | bytes 196616 | tf_op jit(solution)/shard_map/ppermute | solution.py:30
Sparse Core Ops, SparseCore 0:
  171.8 55.1 all-reduce.4

commit v3 on v2

--- a/solution.py
+++ b/solution.py
@@ -11,50 +11,17 @@
 E = 8
 NBY = 2
 NBZ = 16
+HALO = 4
 GROUP = 4
 DIRECT = 4
 SPILL = 16
 PARAMS = pltpu.CompilerParams(vmem_limit_bytes=48 * 1024 * 1024)
 
 
-def with_halo(cells, sides, width):
-    for axis, dim in sides:
-        count = lax.axis_size(axis)
-        ends = count - 1
-        head = lax.slice_in_dim(cells, 0, width, axis=dim)
-        tail = lax.slice_in_dim(cells, cells.shape[dim] - width, cells.shape[dim], axis=dim)
-        cells = jnp.concatenate(
-            [
-                lax.ppermute(tail, axis, [(i, (i + 1) % count) for i in range(ends)]),
-                cells,
-                lax.ppermute(head, axis, [((i + 1) % count, i) for i in range(ends)]),
-            ],
-            axis=dim,
-        )
-    return cells
-
-
 def tap_weights():
     raw_taps = [math.exp(-(offset - 4) * (offset - 4) / 4.5) for offset in range(9)]
     tap_total = sum(raw_taps)
     return [tap_value / tap_total for tap_value in raw_taps]
-
-
-def smooth_axis(padded, axis):
-    weights = tap_weights()
-    length = padded.shape[axis] - 8
-    summed = jnp.zeros(padded.shape[:axis] + (length,) + padded.shape[axis + 1 :], jnp.float32)
-    for offset in range(9):
-        summed = summed + weights[offset] * lax.slice_in_dim(
-            padded, offset, offset + length, axis=axis
-        )
-    return summed
-
-
-def pad_axis(field, axis):
-    widths = [(0, 0)] * field.ndim
-    widths[axis] = (4, 4)
-    return jnp.pad(field, widths)
 
 
 def lookup(indices, table):
@@ -219,7 +186,11 @@
                 for copy in spill_copies(hop):
                     copy.start()
     pack_into(direct_out, devices, DIRECT, 0)
-    for hop in hops:
+    for hop in [0] + hops[:-1]:
+        if further and hop == hops[0]:
+            for first in hops[:-1]:
+                for copy in spill_copies(first):
+                    copy.wait_send()
 
         def begin(turn):
             for copy in direct_copies(hop, turn):
@@ -261,9 +232,6 @@
     for copy in kept:
         copy.wait()
     if further:
-        for hop in range(1, src_count):
-            for copy in spill_copies(hop):
-                copy.wait_send()
         for hop in range(src_count):
             origin = lax.rem(my_src + src_count - hop, src_count)
             each_turn(0, lambda turn: rest_copy(origin, hop, turn).wait())
@@ -362,6 +330,115 @@
     )(notes, *blocks, adjoint)
 
 
+def smooth_body(src_count, vol_count, slab_ref, out_ref, mid, low, high, sends, receives):
+    my_src, my_vol = lax.axis_index("src"), lax.axis_index("vol")
+    length, _, rows, columns = slab_ref.shape
+    mesh_ids = pl.DeviceIdType.MESH
+    has_low, has_high = my_vol > 0, my_vol < vol_count - 1
+
+    def copies(hop, side):
+        plane = lax.rem(my_src + hop, src_count)
+        source, target = {
+            0: (slab_ref, mid),
+            -1: (slab_ref.at[pl.ds(0, HALO)], high),
+            1: (slab_ref.at[pl.ds(length - HALO, HALO)], low),
+        }[side]
+        return pltpu.make_async_remote_copy(
+            src_ref=source,
+            dst_ref=target.at[my_src],
+            send_sem=sends.at[side + 1, hop],
+            recv_sem=receives.at[side + 1, hop],
+            device_id=(plane, lax.rem(my_vol + side + vol_count, vol_count)),
+            device_id_type=mesh_ids,
+        )
+
+    barrier = pltpu.get_barrier_semaphore()
+
+    def greet(side):
+        for hop in range(0 if side else 1, src_count):
+            pl.semaphore_signal(
+                barrier,
+                inc=1,
+                device_id=(lax.rem(my_src + hop, src_count), my_vol + side),
+                device_id_type=mesh_ids,
+            )
+
+    greet(0)
+    pl.when(has_low)(lambda: greet(-1))
+    pl.when(has_high)(lambda: greet(1))
+    sides = jnp.where(has_low, 1, 0) + jnp.where(has_high, 1, 0)
+    pl.semaphore_wait(barrier, src_count - 1 + src_count * sides)
+
+    def start(side):
+        for hop in range(0 if side else 1, src_count):
+            copies(hop, side).start()
+
+    start(0)
+    pl.when(has_low)(lambda: start(-1))
+    pl.when(has_high)(lambda: start(1))
+    mid[my_src] = slab_ref[...]
+
+    @pl.when(jnp.logical_not(has_low))
+    def _():
+        low[...] = jnp.zeros_like(low)
+
+    @pl.when(jnp.logical_not(has_high))
+    def _():
+        high[...] = jnp.zeros_like(high)
+
+    def finish(side):
+        for hop in range(0 if side else 1, src_count):
+            copies(hop, side).wait_send()
+            copies(hop, -side).wait_recv()
+
+    finish(0)
+    pl.when(has_low)(lambda: finish(-1))
+    pl.when(has_high)(lambda: finish(1))
+
+    weights = tap_weights()
+    padded = jnp.concatenate(
+        [sum(part[src] for src in range(src_count)) for part in (low, mid, high)], axis=0
+    )
+    field = sum(weights[at] * padded[at : at + length] for at in range(2 * HALO + 1))
+    edge = jnp.zeros((length, 2, HALO, columns), jnp.float32)
+    padded = jnp.concatenate([edge, field, edge], axis=2)
+    field = sum(weights[at] * padded[:, :, at : at + rows] for at in range(2 * HALO + 1))
+    offset = lax.broadcasted_iota(jnp.int32, (columns, columns), 0)
+    offset = offset - lax.broadcasted_iota(jnp.int32, (columns, columns), 1)
+    taps = sum(
+        jnp.where(offset == at - HALO, weights[at], 0.0) for at in range(2 * HALO + 1)
+    )
+    field = jnp.dot(
+        field.reshape(-1, columns),
+        taps,
+        precision=lax.Precision.HIGHEST,
+        preferred_element_type=jnp.float32,
+    ).reshape(length, 2, rows, columns)
+    for at in range(length):
+        out_ref[:, at] = field[at]
+
+
+def smooth(slab, src_count, vol_count):
+    length, kinds, rows, columns = slab.shape
+    halo = pltpu.VMEM((src_count, HALO, kinds, rows, columns), jnp.float32)
+    return pl.pallas_call(
+        functools.partial(smooth_body, src_count, vol_count),
+        in_specs=[pl.BlockSpec(memory_space=pltpu.VMEM)],
+        out_specs=pl.BlockSpec(memory_space=pltpu.VMEM),
+        out_shape=jax.ShapeDtypeStruct((kinds, length, rows, columns), jnp.float32),
+        scratch_shapes=[
+            pltpu.VMEM((src_count,) + slab.shape, jnp.float32),
+            halo,
+            halo,
+            pltpu.SemaphoreType.DMA((3, src_count)),
+            pltpu.SemaphoreType.DMA((3, src_count)),
+        ],
+        compiler_params=pltpu.CompilerParams(
+            collective_id=1, has_side_effects=True, vmem_limit_bytes=32 * 1024 * 1024
+        ),
+    )(slab)
+
+
 def local(forward, item_tx, item_brick, tx_place, brick_place, adjoint):
     stored = forward.shape[0]
     src_count = lax.axis_size("src")
@@ -421,17 +498,8 @@
 
         raw = lax.cond(jnp.max(notes[:, 15, 0]) > 0, late_pass, lambda: raw)
 
-    slab = (
-        raw.reshape(2, NBY, NBZ, E, E, E)
-        .transpose(0, 3, 1, 4, 2, 5)
-        .reshape(2, E, NBY * E, NBZ * E)
-    )
-    summed = lax.psum(slab, "src")
-    padded = with_halo(summed, (("vol", 1),), 4)
-    field = smooth_axis(padded, 1)
-    for axis in (2, 3):
-        field = smooth_axis(pad_axis(field, axis), axis)
-    return field
+    slab = raw.reshape(2, NBY, NBZ, E, E, E).transpose(3, 0, 1, 4, 2, 5)
+    return smooth(slab.reshape(E, 2, NBY * E, NBZ * E), src_count, vol_count)
 
 
 def solution(mesh):

time: 250 us -> 238 us (0.952)
  Pallas kernels: 153 us -> 225 us
  waiting for transfers between devices: 58.9 us -> 0 us
  between operations: 14.2 us -> 0.81 us
  starting transfers between devices: 7.64 us -> 0 us
    pallas_call x0 -> x1, Pallas kernels: none -> 59.2 us  [smooth(): pl.pallas_call(functools.partial(smooth_body, src_count, vol_count), in_s...]
    psum x1 -> x0, waiting for transfers between devices: 55.3 us -> none  [local(): summed = lax.psum(slab, 'src')]
    pallas_call x1, Pallas kernels: 142 us -> 155 us  [exchange(): pl.pallas_call(functools.partial(exchange_body, src_count, vol_count, fur...]
    ppermute x2 -> x0, starting transfers between devices: 7.64 us -> none  [the longest x1 5.72 us: with_halo(): lax.ppermute(tail, axis, [(i, (i + 1) % count) for i in range(ends)])]
    ppermute x2 -> x0, waiting for transfers between devices: 3.6 us -> none  [the longest x1 3.6 us: with_halo(): lax.ppermute(head, axis, [((i + 1) % count, i) for i in range(ends)])]
  transfers between devices with their start and end apart: 3 -> 0, of which waited for: 2 -> 0; matrix products, arithmetic and copies ran while one was open for 0% -> 0% of each run, Pallas kernels for 0% -> 0%
where the time goes in v3:
time: 238 us; the launch traced here: 237 us
  Pallas kernels  225 us (95%)
  local copies, waits for them, and re-layouts  6.59 us (3%)
  other arithmetic  5.14 us (2%)
    pallas_call x1, Pallas kernels, exchange(): pl.pallas_call(functools.partial(exchange_body, src_count, vol_count, fur...  155 us
    pallas_call x1, Pallas kernels, smooth(): pl.pallas_call(functools.partial(smooth_body, src_count, vol_count), in_s...  59.2 us
    pallas_call x1, Pallas kernels, reduce(): pl.pallas_call(functools.partial(reduce_body, firsts), grid=(channels //...  10.3 us

profile of v3, /device:TPU:3, one launch (start us, length us, event | category | flops | bytes accessed | tf_op | source)
XLA Modules:
  0.0 237.3 jit_solution(4457965331680871156)
XLA Ops:
  0.0 0.8 select_reduce_fusion.3
  0.8 0.8 select_reduce_fusion.1
  1.6 0.2 convert_reduce_fusion.1
  1.8 0.2 convert_reduce_fusion
  2.1 0.1 select_reduce_fusion.2
  2.2 0.1 convert_element_type.29
  2.3 0.7 compare_and_fusion
  3.0 0.1 select_reduce_fusion
  3.2 0.1 convert_element_type.30
  3.3 0.1 sub.34
  3.4 0.6 tile.9.refs_1_
  4.0 1.5 fusion.1.refs_2_
  5.5 0.0 copy-done.1
  5.5 155.3 %shard_map.64 = (bf16[32,9,16,512]{3,2,1,0:T(8,128)(2,1)}, bf16[32,16,128]{2,1,0:T(8,128)(2,1)S(1)}, bf16[32,9,16,512]{3,2,1,0:T(8,128)(2,1)}) custom-call(s32[8,128]{1,0:T(8,128)} %copy-done.1, bf16[4,16,128]{2,1,0:T(8,128)(2,1)} %tile.9.refs_1_, bf16[32,16,128]{2,1,0:T(8,128)(2,1)} %fusion.1.refs_2_, bf16[36,128,512]{2,1,0:T(8,128)(2,1)} %bitcast.50), custom_call_target="tpu_custom_call" | custom-call | tf_op jit(solution)/shard_map/pallas_call | solution.py:267
  160.8 0.6 slice_reduce_fusion
  162.1 0.0 copy-start
  162.1 2.3 copy-done
  164.4 10.3 %shard_map.65 = f32[2,32,512]{2,1,0:T(8,128)S(1)} custom-call(bf16[32,16,128]{2,1,0:T(8,128)(2,1)S(1)} %get-tuple-element.57.notes_ref, bf16[32,9,16,512]{3,2,1,0:T(8,128)(2,1)S(1)} %copy-done, bf16[32,9,16,512]{3,2,1,0:T(8,128)(2,1)} %get-tuple-element.59.refs_1_, bf16[4,36,32,512]{3,2,1,0:T(8,128)(2,1)} %bitcast.46), custom_call_target="tpu_custom_call" | custom-call | tf_op jit(solution)/shard_map/pallas_call | solution.py:320
  174.7 0.2 copy.10
  174.9 0.6 reshape.361
  175.5 0.9 copy.11
  176.4 1.0 reshape.362.slab_ref
  177.4 59.2 %shard_map.66 = f32[2,8,16,128]{3,2,1,0:T(8,128)S(1)} custom-call(f32[8,2,16,128]{3,2,1,0:T(8,128)S(1)} %reshape.362.slab_ref), custom_call_target="tpu_custom_call" | custom-call | tf_op jit(solution)/shard_map/pallas_call | solution.py:424
  236.6 0.7 copy.19
  (12 shorter events, 0.1 us)
Async XLA Ops:
  3.2 2.3 copy-start.1
  162.1 2.3 copy-start

commit v4 on v3

--- a/solution.py
+++ b/solution.py
@@ -186,52 +186,70 @@
                 for copy in spill_copies(hop):
                     copy.start()
     pack_into(direct_out, devices, DIRECT, 0)
-    for hop in [0] + hops[:-1]:
-        if further and hop == hops[0]:
-            for first in hops[:-1]:
-                for copy in spill_copies(first):
-                    copy.wait_send()
-
-        def begin(turn):
-            for copy in direct_copies(hop, turn):
-                copy.start()
-
-        each_turn(hop, begin)
     kept = [
         pltpu.make_async_copy(direct_out.at[me], direct_in.at[me], own.at[0]),
         pltpu.make_async_copy(notes_ref.at[me], notes_in.at[me], own.at[1]),
     ]
-    if further:
-        for hop in sorted(range(src_count), key=lambda hop: (min(hop, src_count - hop), hop)):
-            origin = lax.rem(my_src + src_count - hop, src_count)
-            if hop:
-                for copy in spill_copies(hop):
-                    copy.wait_recv()
-            codes, spill = (codes_in, spill_in) if hop else (codes_ref, spill_out)
-            code = codes[origin].astype(jnp.float32)[0:1, : GROUP * SPILL].astype(jnp.int32)
-            number, channel = row_ids((vol_count * GROUP * further, GROUP * SPILL), further)
-            table = pick_table(number == code, channel, SPILL)
-
-            def repack(group, carry):
-                moved = jnp.dot(table, spill[origin, group], preferred_element_type=jnp.float32)
-                moved = moved.astype(jnp.bfloat16)
-                rest_out[origin, :, group] = moved.reshape(vol_count, GROUP * further, width)
-                return carry
-
-            lax.fori_loop(0, groups, repack, 0)
-            each_turn(0, lambda turn: rest_copy(origin, hop, turn).start())
-            kept.append(
-                pltpu.make_async_copy(
-                    rest_out.at[origin, my_vol],
-                    rest_in.at[origin * vol_count + my_vol],
-                    own.at[2 + hop],
-                )
+
+    def send_turns(first, last):
+        def body(turn, carry):
+            for hop in hops:
+                for copy in direct_copies(hop, turn):
+                    copy.start()
+            return carry
+
+        if first == 0:
+            for hop in hops[:-1]:
+                for copy in direct_copies(hop, 0):
+                    copy.start()
+        lax.fori_loop(max(first, 1), last, body, 0)
+
+    def send_rest(hop):
+        origin = lax.rem(my_src + src_count - hop, src_count)
+        if hop:
+            for copy in spill_copies(hop):
+                copy.wait_recv()
+        codes, spill = (codes_in, spill_in) if hop else (codes_ref, spill_out)
+        code = codes[origin].astype(jnp.float32)[0:1, : GROUP * SPILL].astype(jnp.int32)
+        number, channel = row_ids((vol_count * GROUP * further, GROUP * SPILL), further)
+        table = pick_table(number == code, channel, SPILL)
+
+        def repack(group, carry):
+            moved = jnp.dot(table, spill[origin, group], preferred_element_type=jnp.float32)
+            moved = moved.astype(jnp.bfloat16)
+            rest_out[origin, :, group] = moved.reshape(vol_count, GROUP * further, width)
+            return carry
+
+        lax.fori_loop(0, groups, repack, 0)
+        each_turn(0, lambda turn: rest_copy(origin, hop, turn).start())
+        kept.append(
+            pltpu.make_async_copy(
+                rest_out.at[origin, my_vol],
+                rest_in.at[origin * vol_count + my_vol],
+                own.at[2 + hop],
             )
+        )
+
+    turn = vol_count * 5 // 8 if further else vol_count
+    if further:
+        send_rest(0)
+    send_turns(0, turn)
+    if further:
+        for hop in sorted(range(1, src_count), key=lambda hop: (min(hop, src_count - hop), hop)):
+            send_rest(hop)
+            if turn < vol_count:
+                send_turns(turn, turn + 1)
+                turn += 1
+    if turn < vol_count:
+        send_turns(turn, vol_count)
     for copy in kept:
         copy.start()
     for copy in kept:
         copy.wait()
     if further:
+        for hop in range(1, src_count):
+            for copy in spill_copies(hop):
+                copy.wait_send()
         for hop in range(src_count):
             origin = lax.rem(my_src + src_count - hop, src_count)
             each_turn(0, lambda turn: rest_copy(origin, hop, turn).wait())
@@ -330,18 +348,20 @@
     )(notes, *blocks, adjoint)
 
 
-def smooth_body(src_count, vol_count, slab_ref, out_ref, mid, low, high, sends, receives):
+def smooth_body(src_count, vol_count, slab_ref, out_ref, mid, low, high, done, sends, receives):
     my_src, my_vol = lax.axis_index("src"), lax.axis_index("vol")
-    length, _, rows, columns = slab_ref.shape
+    _, length, part_rows, columns = slab_ref.shape
+    kinds, _, rows, _ = out_ref.shape
     mesh_ids = pl.DeviceIdType.MESH
     has_low, has_high = my_vol > 0, my_vol < vol_count - 1
+    gather = 3
 
     def copies(hop, side):
         plane = lax.rem(my_src + hop, src_count)
         source, target = {
-            0: (slab_ref, mid),
-            -1: (slab_ref.at[pl.ds(0, HALO)], high),
-            1: (slab_ref.at[pl.ds(length - HALO, HALO)], low),
+            0: (slab_ref.at[plane], mid),
+            -1: (slab_ref.at[plane, pl.ds(0, HALO)], high),
+            1: (slab_ref.at[plane, pl.ds(length - HALO, HALO)], low),
         }[side]
         return pltpu.make_async_remote_copy(
             src_ref=source,
@@ -352,6 +372,16 @@
             device_id_type=mesh_ids,
         )
 
+    def gather_copy(hop):
+        return pltpu.make_async_remote_copy(
+            src_ref=done.at[my_src],
+            dst_ref=done.at[my_src],
+            send_sem=sends.at[gather, hop],
+            recv_sem=receives.at[gather, hop],
+            device_id=(lax.rem(my_src + hop, src_count), my_vol),
+            device_id_type=mesh_ids,
+        )
+
     barrier = pltpu.get_barrier_semaphore()
 
     def greet(side):
@@ -376,7 +406,7 @@
     start(0)
     pl.when(has_low)(lambda: start(-1))
     pl.when(has_high)(lambda: start(1))
-    mid[my_src] = slab_ref[...]
+    mid[my_src] = slab_ref[my_src]
 
     @pl.when(jnp.logical_not(has_low))
     def _():
@@ -386,52 +416,69 @@
     def _():
         high[...] = jnp.zeros_like(high)
 
-    def finish(side):
-        for hop in range(0 if side else 1, src_count):
-            copies(hop, side).wait_send()
-            copies(hop, -side).wait_recv()
-
-    finish(0)
-    pl.when(has_low)(lambda: finish(-1))
-    pl.when(has_high)(lambda: finish(1))
-
     weights = tap_weights()
-    padded = jnp.concatenate(
-        [sum(part[src] for src in range(src_count)) for part in (low, mid, high)], axis=0
-    )
-    field = sum(weights[at] * padded[at : at + length] for at in range(2 * HALO + 1))
-    edge = jnp.zeros((length, 2, HALO, columns), jnp.float32)
-    padded = jnp.concatenate([edge, field, edge], axis=2)
-    field = sum(weights[at] * padded[:, :, at : at + rows] for at in range(2 * HALO + 1))
     offset = lax.broadcasted_iota(jnp.int32, (columns, columns), 0)
     offset = offset - lax.broadcasted_iota(jnp.int32, (columns, columns), 1)
     taps = sum(
         jnp.where(offset == at - HALO, weights[at], 0.0) for at in range(2 * HALO + 1)
     )
+
+    def arrive(side):
+        for hop in range(0 if side else 1, src_count):
+            copies(hop, -side).wait_recv()
+
+    arrive(0)
+    pl.when(has_low)(lambda: arrive(-1))
+    pl.when(has_high)(lambda: arrive(1))
+    padded = jnp.concatenate(
+        [sum(part[src] for src in range(src_count)) for part in (low, mid, high)], axis=0
+    )
+    field = sum(weights[at] * padded[at : at + length] for at in range(2 * HALO + 1))
     field = jnp.dot(
         field.reshape(-1, columns),
         taps,
         precision=lax.Precision.HIGHEST,
         preferred_element_type=jnp.float32,
-    ).reshape(length, 2, rows, columns)
-    for at in range(length):
-        out_ref[:, at] = field[at]
+    )
+    done[my_src] = field.reshape(length, part_rows, columns)
+    for hop in range(1, src_count):
+        gather_copy(hop).start()
+
+    def leave(side):
+        for hop in range(0 if side else 1, src_count):
+            copies(hop, side).wait_send()
+
+    leave(0)
+    pl.when(has_low)(lambda: leave(-1))
+    pl.when(has_high)(lambda: leave(1))
+    for hop in range(1, src_count):
+        gather_copy(hop).wait()
+    edge = jnp.zeros((length, HALO, columns), jnp.float32)
+    share = src_count // kinds
+    for kind in range(kinds):
+        parts = [done[kind * share + at] for at in range(share)]
+        padded = jnp.concatenate([edge] + parts + [edge], axis=1)
+        out_ref[kind] = sum(weights[at] * padded[:, at : at + rows] for at in range(2 * HALO + 1))
 
 
 def smooth(slab, src_count, vol_count):
     length, kinds, rows, columns = slab.shape
-    halo = pltpu.VMEM((src_count, HALO, kinds, rows, columns), jnp.float32)
+    part = (length, kinds * rows // src_count, columns)
+    slab = slab.reshape(length, src_count, part[1], columns).swapaxes(0, 1)
+    whole = pltpu.VMEM((src_count,) + part, jnp.float32)
+    halo = pltpu.VMEM((src_count, HALO) + part[1:], jnp.float32)
     return pl.pallas_call(
         functools.partial(smooth_body, src_count, vol_count),
         in_specs=[pl.BlockSpec(memory_space=pltpu.VMEM)],
         out_specs=pl.BlockSpec(memory_space=pltpu.VMEM),
         out_shape=jax.ShapeDtypeStruct((kinds, length, rows, columns), jnp.float32),
         scratch_shapes=[
-            pltpu.VMEM((src_count,) + slab.shape, jnp.float32),
+            whole,
             halo,
             halo,
-            pltpu.SemaphoreType.DMA((3, src_count)),
-            pltpu.SemaphoreType.DMA((3, src_count)),
+            whole,
+            pltpu.SemaphoreType.DMA((4, src_count)),
+            pltpu.SemaphoreType.DMA((4, src_count)),
         ],
         compiler_params=pltpu.CompilerParams(
             collective_id=1, has_side_effects=True, vmem_limit_bytes=32 * 1024 * 1024

time: 238 us -> 205 us (0.86)
  Pallas kernels: 225 us -> 192 us
    pallas_call x1, Pallas kernels: 59.2 us -> 15.6 us  [smooth(): pl.pallas_call(functools.partial(smooth_body, src_count, vol_count), in_s...]
    pallas_call x1, Pallas kernels: 155 us -> 166 us  [exchange(): pl.pallas_call(functools.partial(exchange_body, src_count, vol_count, fur...]
where the time goes in v4:
time: 205 us; the launch traced here: 204 us
  Pallas kernels  192 us (94%)
  local copies, waits for them, and re-layouts  6.59 us (3%)
  other arithmetic  5.14 us (3%)
    pallas_call x1, Pallas kernels, exchange(): pl.pallas_call(functools.partial(exchange_body, src_count, vol_count, fur...  166 us
    pallas_call x1, Pallas kernels, smooth(): pl.pallas_call(functools.partial(smooth_body, src_count, vol_count), in_s...  15.6 us
    pallas_call x1, Pallas kernels, reduce(): pl.pallas_call(functools.partial(reduce_body, firsts), grid=(channels //...  10.3 us

profile of v4, /device:TPU:3, one launch (start us, length us, event | category | flops | bytes accessed | tf_op | source)
XLA Modules:
  0.0 204.2 jit_solution(7078039179841461488)
XLA Ops:
  0.0 0.8 select_reduce_fusion.3
  0.8 0.8 select_reduce_fusion.1
  1.6 0.2 convert_reduce_fusion.1
  1.8 0.2 convert_reduce_fusion
  2.1 0.1 select_reduce_fusion.2
  2.2 0.1 convert_element_type.29
  2.3 0.7 compare_and_fusion
  3.0 0.1 select_reduce_fusion
  3.2 0.1 convert_element_type.30
  3.3 0.1 sub.34
  3.4 0.6 tile.9.refs_1_
  4.0 1.5 fusion.1.refs_2_
  5.5 0.0 copy-done.1
  5.5 165.8 %shard_map.64 = (bf16[32,9,16,512]{3,2,1,0:T(8,128)(2,1)}, bf16[32,16,128]{2,1,0:T(8,128)(2,1)S(1)}, bf16[32,9,16,512]{3,2,1,0:T(8,128)(2,1)}) custom-call(s32[8,128]{1,0:T(8,128)} %copy-done.1, bf16[4,16,128]{2,1,0:T(8,128)(2,1)} %tile.9.refs_1_, bf16[32,16,128]{2,1,0:T(8,128)(2,1)} %fusion.1.refs_2_, bf16[36,128,512]{2,1,0:T(8,128)(2,1)} %bitcast.54), custom_call_target="tpu_custom_call" | custom-call | tf_op jit(solution)/shard_map/pallas_call | solution.py:285
  171.3 0.6 slice_reduce_fusion
  172.6 0.0 copy-start
  172.6 2.3 %copy-done = bf16[32,9,16,512]{3,2,1,0:T(8,128)(2,1)S(1)} copy-done((bf16[32,9,16,512]{3,2,1,0:T(8,128)(2,1)S(1)}, bf16[32,9,16,512]{3,2,1,0:T(8,128)(2,1)}, u32[]{:S(2)}) %copy-start) | copy-done | bytes 4718616
  174.9 10.3 %shard_map.65 = f32[2,32,512]{2,1,0:T(8,128)S(1)} custom-call(bf16[32,16,128]{2,1,0:T(8,128)(2,1)S(1)} %get-tuple-element.57.notes_ref, bf16[32,9,16,512]{3,2,1,0:T(8,128)(2,1)S(1)} %copy-done, bf16[32,9,16,512]{3,2,1,0:T(8,128)(2,1)} %get-tuple-element.59.refs_1_, bf16[4,36,32,512]{3,2,1,0:T(8,128)(2,1)} %bitcast.50), custom_call_target="tpu_custom_call" | custom-call | tf_op jit(solution)/shard_map/pallas_call | solution.py:338
  185.2 0.2 copy.11
  185.4 0.6 reshape.358
  186.1 0.9 copy.14
  186.9 1.0 reshape.360
  187.9 15.6 %shard_map.66 = f32[2,8,16,128]{3,2,1,0:T(8,128)S(1)} custom-call(f32[4,8,8,128]{3,2,1,0:T(8,128)S(1)} %bitcast.49), custom_call_target="tpu_custom_call" | custom-call | tf_op jit(solution)/shard_map/pallas_call | solution.py:470
  203.6 0.7 copy.23
  (12 shorter events, 0.1 us)
Async XLA Ops:
  3.2 2.3 %copy-start.1 = (s32[8,128]{1,0:T(8,128)}, s32[8,128]{1,0:T(8,128)S(1)}, u32[]{:S(2)}) copy-start(s32[8,128]{1,0:T(8,128)S(1)} %scatter.9.refs_0_) | copy-start | bytes 12292
  172.6 2.3 %copy-start = (bf16[32,9,16,512]{3,2,1,0:T(8,128)(2,1)S(1)}, bf16[32,9,16,512]{3,2,1,0:T(8,128)(2,1)}, u32[]{:S(2)}) copy-start(bf16[32,9,16,512]{3,2,1,0:T(8,128)(2,1)} %get-tuple-element.58.refs_0_) | copy-start | bytes 14155780

commit v5 on v4

--- a/solution.py
+++ b/solution.py
@@ -15,6 +15,7 @@
 GROUP = 4
 DIRECT = 4
 SPILL = 16
+POOL = 20
 PARAMS = pltpu.CompilerParams(vmem_limit_bytes=48 * 1024 * 1024)
 
 
@@ -82,9 +83,12 @@
 
 def exchange_body(src_count, vol_count, further, *refs):
     if further:
-        (slots_ref, codes_ref, notes_ref, cells_ref, direct_in, notes_in, rest_in) = refs[:7]
-        (direct_out, sends, receives, own, spill_out, spill_in, codes_in, rest_out) = refs[7:15]
-        (spill_sends, spill_receives, rest_sends, rest_receives) = refs[15:]
+        (slots_ref, codes_ref, pool_codes_ref, notes_ref, cells_ref) = refs[:5]
+        (direct_in, notes_in, rest_in) = refs[5:8]
+        (direct_out, sends, receives, own, spill_out, spill_in, codes_in, rest_out) = refs[8:16]
+        (pool_out, pool_in, pool_codes_in, relay_out) = refs[16:20]
+        (spill_sends, spill_receives, rest_sends, rest_receives) = refs[20:]
+        assert src_count == 4
     else:
         (slots_ref, notes_ref, cells_ref, direct_in, notes_in) = refs[:5]
         (direct_out, sends, receives, own) = refs[5:]
@@ -124,21 +128,39 @@
 
         lax.fori_loop(0, groups, pack_group, 0)
 
-    def spill_copies(hop):
-        plane = lax.rem(my_src + hop, src_count)
-        return [
-            pltpu.make_async_remote_copy(
-                src_ref=source.at[plane],
-                dst_ref=target.at[my_src],
-                send_sem=spill_sends.at[kind, hop],
-                recv_sem=spill_receives.at[kind, hop],
-                device_id=(plane, my_vol),
-                device_id_type=mesh_ids,
-            )
-            for kind, (source, target) in enumerate(
-                ((codes_ref, codes_in), (spill_out, spill_in))
-            )
-        ]
+    half = my_src // 2
+    parity = lax.rem(my_src, 2)
+    near = my_src + 1 - 2 * parity
+    inner, outer, across = 2 - half, 3 - 3 * half, 2 - 2 * half
+    is_inner = (my_src == 1) | (my_src == 2)
+
+    def spill_copy(at, source, target, plane):
+        return pltpu.make_async_remote_copy(
+            src_ref=source,
+            dst_ref=target,
+            send_sem=spill_sends.at[at],
+            recv_sem=spill_receives.at[at],
+            device_id=(plane, my_vol),
+            device_id_type=mesh_ids,
+        )
+
+    def near_copy():
+        return spill_copy(0, spill_out.at[near], spill_in.at[my_src], near)
+
+    def near_codes():
+        return spill_copy(1, codes_ref.at[near], codes_in.at[my_src], near)
+
+    def outer_codes(which):
+        return spill_copy(2 + which, codes_ref.at[outer], codes_in.at[my_src], outer)
+
+    def pool_copy(which):
+        return spill_copy(4 + which, pool_out.at[0], pool_in.at[parity], inner)
+
+    def pool_codes(which):
+        return spill_copy(6 + which, pool_codes_ref, pool_codes_in.at[parity], inner)
+
+    def relay_copy(which):
+        return spill_copy(8 + which, relay_out.at[which], spill_in.at[across + which], near)
 
     def direct_copies(hop, turn):
         plane = lax.rem(my_src + hop, src_count)
@@ -158,13 +180,13 @@
             )
         ]
 
-    def rest_copy(origin, hop, turn):
+    def rest_copy(origin, turn):
         column = lax.rem(my_vol + turn, vol_count)
         return pltpu.make_async_remote_copy(
             src_ref=rest_out.at[origin, column],
             dst_ref=rest_in.at[origin * vol_count + my_vol],
-            send_sem=rest_sends.at[hop, turn],
-            recv_sem=rest_receives.at[hop, turn],
+            send_sem=rest_sends.at[origin, turn],
+            recv_sem=rest_receives.at[origin, turn],
             device_id=(my_src, column),
             device_id_type=mesh_ids,
         )
@@ -178,13 +200,15 @@
 
     hops = sorted(range(src_count), key=lambda hop: (hop == 0, abs(2 * hop - src_count), hop))
     if further:
+        pack_into(pool_out, 1, POOL, 2)
         pack_into(spill_out, src_count, SPILL, 1)
     pl.semaphore_wait(barrier, devices - 1)
     if further:
-        for hop in hops:
-            if hop:
-                for copy in spill_copies(hop):
-                    copy.start()
+        pool_codes(parity).start()
+        pool_copy(parity).start()
+        near_codes().start()
+        near_copy().start()
+        outer_codes(parity).start()
     pack_into(direct_out, devices, DIRECT, 0)
     kept = [
         pltpu.make_async_copy(direct_out.at[me], direct_in.at[me], own.at[0]),
@@ -204,55 +228,85 @@
                     copy.start()
         lax.fori_loop(max(first, 1), last, body, 0)
 
-    def send_rest(hop):
-        origin = lax.rem(my_src + src_count - hop, src_count)
-        if hop:
-            for copy in spill_copies(hop):
-                copy.wait_recv()
-        codes, spill = (codes_in, spill_in) if hop else (codes_ref, spill_out)
-        code = codes[origin].astype(jnp.float32)[0:1, : GROUP * SPILL].astype(jnp.int32)
-        number, channel = row_ids((vol_count * GROUP * further, GROUP * SPILL), further)
-        table = pick_table(number == code, channel, SPILL)
-
-        def repack(group, carry):
-            moved = jnp.dot(table, spill[origin, group], preferred_element_type=jnp.float32)
-            moved = moved.astype(jnp.bfloat16)
-            rest_out[origin, :, group] = moved.reshape(vol_count, GROUP * further, width)
+    def code_row(codes, row, slots):
+        codes = codes.astype(jnp.float32)[row : row + 1, : GROUP * slots]
+        return codes.astype(jnp.int32)
+
+    def repack(code, parts, slots, held, chunk, out):
+        number, channel = row_ids((parts * GROUP * slots, GROUP * held), slots)
+        table = pick_table(number == code, channel, held)
+
+        def body(group, carry):
+            moved = jnp.dot(table, chunk[group], preferred_element_type=jnp.float32)
+            out[:, group] = moved.astype(jnp.bfloat16).reshape(parts, GROUP * slots, width)
             return carry
 
-        lax.fori_loop(0, groups, repack, 0)
-        each_turn(0, lambda turn: rest_copy(origin, hop, turn).start())
-        kept.append(
-            pltpu.make_async_copy(
-                rest_out.at[origin, my_vol],
-                rest_in.at[origin * vol_count + my_vol],
-                own.at[2 + hop],
+        lax.fori_loop(0, groups, body, 0)
+
+    def send_rest(origin, code, held, chunk):
+        repack(code, vol_count, further, held, chunk, rest_out.at[origin])
+        each_turn(0, lambda turn: rest_copy(origin, turn).start())
+
+    if further:
+        send_rest(my_src, code_row(codes_ref[my_src], 0, SPILL), SPILL, spill_out.at[my_src])
+        first, second = vol_count // 2, vol_count * 3 // 4
+        send_turns(0, first)
+        near_codes().wait_recv()
+        near_copy().wait_recv()
+        send_rest(near, code_row(codes_in[near], 0, SPILL), SPILL, spill_in.at[near])
+
+        @pl.when(is_inner)
+        def _():
+            for which in range(2):
+                pool_codes(which).wait_recv()
+                pool_copy(which).wait_recv()
+                code = code_row(pool_codes_in[which], 8, POOL)
+                relay = relay_out.at[pl.ds(which, 1)]
+                repack(code, 1, SPILL, POOL, pool_in.at[which], relay)
+                relay_copy(which).start()
+            for which in range(2):
+                code = code_row(pool_codes_in[which], 0, POOL)
+                send_rest(across + which, code, POOL, pool_in.at[which])
+
+        send_turns(first, second)
+
+        @pl.when(jnp.logical_not(is_inner))
+        def _():
+            for which in range(2):
+                origin = across + which
+                outer_codes(which).wait_recv()
+                relay_copy(which).wait_recv()
+                send_rest(origin, code_row(codes_in[origin], 0, SPILL), SPILL, spill_in.at[origin])
+
+        send_turns(second, vol_count)
+        for origin in range(src_count):
+            kept.append(
+                pltpu.make_async_copy(
+                    rest_out.at[origin, my_vol],
+                    rest_in.at[origin * vol_count + my_vol],
+                    own.at[2 + origin],
+                )
             )
-        )
-
-    turn = vol_count * 5 // 8 if further else vol_count
-    if further:
-        send_rest(0)
-    send_turns(0, turn)
-    if further:
-        for hop in sorted(range(1, src_count), key=lambda hop: (min(hop, src_count - hop), hop)):
-            send_rest(hop)
-            if turn < vol_count:
-                send_turns(turn, turn + 1)
-                turn += 1
-    if turn < vol_count:
-        send_turns(turn, vol_count)
+    else:
+        send_turns(0, vol_count)
     for copy in kept:
         copy.start()
     for copy in kept:
         copy.wait()
     if further:
-        for hop in range(1, src_count):
-            for copy in spill_copies(hop):
-                copy.wait_send()
-        for hop in range(src_count):
-            origin = lax.rem(my_src + src_count - hop, src_count)
-            each_turn(0, lambda turn: rest_copy(origin, hop, turn).wait())
+        pool_codes(parity).wait_send()
+        pool_copy(parity).wait_send()
+        near_codes().wait_send()
+        near_copy().wait_send()
+        outer_codes(parity).wait_send()
+
+        @pl.when(is_inner)
+        def _():
+            for which in range(2):
+                relay_copy(which).wait_send()
+
+        for origin in range(src_count):
+            each_turn(0, lambda turn: rest_copy(origin, turn).wait())
     for hop in hops:
 
         def finish(turn):
@@ -262,13 +316,13 @@
         each_turn(hop, finish)
 
 
-def exchange(slots, codes, notes, cells, src_count, vol_count, further):
+def exchange(slots, codes, pool_codes, notes, cells, src_count, vol_count, further):
     channels, _, width = cells.shape
     groups = channels // GROUP
     devices = src_count * vol_count
     kind = cells.dtype
     chunk = (groups, GROUP * DIRECT, width)
-    inputs = [slots] + ([codes] if further else []) + [notes, cells]
+    inputs = [slots] + ([codes, pool_codes] if further else []) + [notes, cells]
     outputs = [(devices,) + chunk, notes.shape] + ([(devices,) + chunk] if further else [])
     dma = pltpu.SemaphoreType.DMA
     scratch = [
@@ -281,7 +335,11 @@
         spill = pltpu.VMEM((src_count, groups, GROUP * SPILL, width), kind)
         scratch += [spill, spill, pltpu.VMEM(codes.shape, codes.dtype)]
         scratch += [pltpu.VMEM((src_count, vol_count) + chunk, kind)]
-        scratch += [dma((2, src_count))] * 2 + [dma((src_count, vol_count))] * 2
+        rows = (groups, GROUP * POOL, width)
+        scratch += [pltpu.VMEM((1,) + rows, kind), pltpu.VMEM((2,) + rows, kind)]
+        scratch += [pltpu.VMEM((2,) + pool_codes.shape, kind)]
+        scratch += [pltpu.VMEM((2, groups, GROUP * SPILL, width), kind)]
+        scratch += [dma((10,))] * 2 + [dma((src_count, vol_count))] * 2
     return pl.pallas_call(
         functools.partial(exchange_body, src_count, vol_count, further),
         in_specs=[pl.BlockSpec(memory_space=pltpu.VMEM)] * len(inputs),
@@ -513,6 +571,11 @@
     before = earlier & spilled[None, :] & (plane[:, None] == plane[None, :])
     spill_rank = jnp.sum(before, axis=1, dtype=jnp.int32)
     late = spilled & (spill_rank >= SPILL)
+    half = src_count // 2
+    far = spilled & ~late & (plane // half != lax.axis_index("src") // half)
+    pool_rank = jnp.sum(earlier & far[None, :], axis=1, dtype=jnp.int32)
+    late = late | (far & (pool_rank >= POOL))
+    far = far & ~late
 
     channel_major = forward.transpose(1, 0, 2)
     adjoint_major = adjoint.transpose(0, 2, 1, 3)
@@ -525,11 +588,19 @@
     direct_slot = jnp.where(spilled, -1, owner * DIRECT + rank)
     spill_slot = jnp.where(spilled & ~late, plane * SPILL + spill_rank, -1)
     slots = jnp.zeros((8, stored), jnp.int32).at[0].set(direct_slot).at[1].set(spill_slot)
-    codes = None
+    codes = pool_codes = None
     if further:
         codes = place(spill_slot, column * further + rank - DIRECT, src_count * SPILL)
         codes = jnp.tile(codes.reshape(src_count, 1, SPILL), (1, 16, 128 // SPILL)).astype(kind)
-    moved = exchange(slots, codes, notes, channel_major, src_count, vol_count, further)
+        pool_slot = jnp.where(far, pool_rank, -1)
+        slots = slots.at[2].set(pool_slot)
+        is_inner = (plane == 1) | (plane == 2)
+        to_rest = place(pool_slot, jnp.where(is_inner, column * further + rank - DIRECT, -1), POOL)
+        to_relay = place(pool_slot, jnp.where(is_inner, -1, spill_rank), POOL)
+        pool_codes = jnp.stack([to_rest, to_relay])[:, None, :]
+        pool_codes = jnp.tile(pool_codes, (1, 8, 128 // POOL)).reshape(16, -1)
+        pool_codes = jnp.pad(pool_codes, ((0, 0), (0, 128 - pool_codes.shape[1]))).astype(kind)
+    moved = exchange(slots, codes, pool_codes, notes, channel_major, src_count, vol_count, further)
     notes = moved[1]
     firsts = (0, DIRECT) if further else (0,)
     raw = reduce(notes, firsts, [moved[0]] + list(moved[2:]), adjoint_major)

time: 205 us -> 189 us (0.922)
  Pallas kernels: 192 us -> 174 us
    pallas_call x1, Pallas kernels: 166 us -> 151 us  [exchange(): pl.pallas_call(functools.partial(exchange_body, src_count, vol_count, fur...]
    pallas_call x1, Pallas kernels: 15.6 us -> 12.5 us  [smooth(): pl.pallas_call(functools.partial(smooth_body, src_count, vol_count), in_s...]
where the time goes in v5:
time: 189 us; the launch traced here: 187 us
  Pallas kernels  174 us (92%)
  local copies, waits for them, and re-layouts  7.32 us (4%)
  other arithmetic  5.41 us (3%)
    pallas_call x1, Pallas kernels, exchange(): pl.pallas_call(functools.partial(exchange_body, src_count, vol_count, fur...  151 us
    pallas_call x1, Pallas kernels, smooth(): pl.pallas_call(functools.partial(smooth_body, src_count, vol_count), in_s...  12.5 us
    pallas_call x1, Pallas kernels, reduce(): pl.pallas_call(functools.partial(reduce_body, firsts), grid=(channels //...  10.3 us

profile of v5, /device:TPU:3, one launch (start us, length us, event | category | flops | bytes accessed | tf_op | source)
XLA Modules:
  0.0 187.2 jit_solution(10854015493986930754)
XLA Ops:
  0.0 0.8 select_reduce_fusion.5
  0.8 0.8 select_reduce_fusion.1
  1.6 0.2 convert_reduce_fusion.2
  1.8 0.2 convert_reduce_fusion.1
  2.0 0.1 convert_reduce_fusion
  2.2 0.7 fusion.11
  2.9 0.1 select_reduce_fusion.2
  3.1 0.2 select_reduce_fusion
  3.3 0.1 select_reduce_fusion.4
  3.5 0.1 convert_element_type.35
  3.7 0.6 tile.16.refs_1_
  4.3 0.1 tile.18
  4.4 0.6 pad.12.refs_2_
  5.0 1.5 fusion.1.refs_3_
  6.5 150.9 %shard_map.64 = (bf16[32,9,16,512]{3,2,1,0:T(8,128)(2,1)}, bf16[32,16,128]{2,1,0:T(8,128)(2,1)S(1)}, bf16[32,9,16,512]{3,2,1,0:T(8,128)(2,1)}) custom-call(s32[8,128]{1,0:T(8,128)} %copy-done.1, bf16[4,16,128]{2,1,0:T(8,128)(2,1)} %tile.16.refs_1_, bf16[16,128]{1,0:T(8,128)(2,1)} %pad.12.refs_2_, bf16[32,16,128]{2,1,0:T(8,128)(2,1)} %fusion.1.refs_3_, ...), custom_call_target="tpu_custom_call" | custom-call | tf_op jit(solution)/shard_map/pallas_call | solution.py:343
  157.4 0.6 slice_reduce_fusion
  158.7 2.3 %copy-done = bf16[32,9,16,512]{3,2,1,0:T(8,128)(2,1)S(1)} copy-done((bf16[32,9,16,512]{3,2,1,0:T(8,128)(2,1)S(1)}, bf16[32,9,16,512]{3,2,1,0:T(8,128)(2,1)}, u32[]{:S(2)}) %copy-start) | copy-done | bytes 4718616
  161.0 10.3 %shard_map.65 = f32[2,32,512]{2,1,0:T(8,128)S(1)} custom-call(bf16[32,16,128]{2,1,0:T(8,128)(2,1)S(1)} %get-tuple-element.69.notes_ref, bf16[32,9,16,512]{3,2,1,0:T(8,128)(2,1)S(1)} %copy-done, bf16[32,9,16,512]{3,2,1,0:T(8,128)(2,1)} %get-tuple-element.71.refs_1_, bf16[4,36,32,512]{3,2,1,0:T(8,128)(2,1)} %bitcast.98), custom_call_target="tpu_custom_call" | custom-call | tf_op jit(solution)/shard_map/pallas_call | solution.py:396
  171.3 0.2 copy.11
  171.5 0.6 reshape.527
  172.1 0.9 copy.14
  173.0 1.0 reshape.529
  174.0 12.5 %shard_map.66 = f32[2,8,16,128]{3,2,1,0:T(8,128)S(1)} custom-call(f32[4,8,8,128]{3,2,1,0:T(8,128)S(1)} %bitcast.97), custom_call_target="tpu_custom_call" | custom-call | tf_op jit(solution)/shard_map/pallas_call | solution.py:528
  186.6 0.7 copy.24
  (21 shorter events, 0.4 us)
Async XLA Ops:
  3.5 3.0 %copy-start.1 = (s32[8,128]{1,0:T(8,128)}, s32[8,128]{1,0:T(8,128)S(1)}, u32[]{:S(2)}) copy-start(s32[8,128]{1,0:T(8,128)S(1)} %scatter.14.refs_0_) | copy-start | bytes 12292
  158.7 2.3 %copy-start = (bf16[32,9,16,512]{3,2,1,0:T(8,128)(2,1)S(1)}, bf16[32,9,16,512]{3,2,1,0:T(8,128)(2,1)}, u32[]{:S(2)}) copy-start(bf16[32,9,16,512]{3,2,1,0:T(8,128)(2,1)} %get-tuple-element.70.refs_0_) | copy-start | bytes 14155780

commit v6 on v5

--- a/solution.py
+++ b/solution.py
@@ -16,7 +16,7 @@
 DIRECT = 4
 SPILL = 16
 POOL = 20
-PARAMS = pltpu.CompilerParams(vmem_limit_bytes=48 * 1024 * 1024)
+PARAMS = pltpu.CompilerParams(vmem_limit_bytes=60 * 1024 * 1024)
 
 
 def tap_weights():
@@ -201,11 +201,11 @@
     hops = sorted(range(src_count), key=lambda hop: (hop == 0, abs(2 * hop - src_count), hop))
     if further:
         pack_into(pool_out, 1, POOL, 2)
-        pack_into(spill_out, src_count, SPILL, 1)
     pl.semaphore_wait(barrier, devices - 1)
     if further:
         pool_codes(parity).start()
         pool_copy(parity).start()
+        pack_into(spill_out, src_count, SPILL, 1)
         near_codes().start()
         near_copy().start()
         outer_codes(parity).start()

time: 189 us -> 187 us (0.989)
  local copies, waits for them, and re-layouts: 7.32 us -> 4.99 us
    unnamed x5 -> x3, local copies, waits for them, and re-layouts: 2.99 us -> 0.66 us
where the time goes in v6:
time: 187 us; the launch traced here: 184 us
  Pallas kernels  173 us (93%)
  other arithmetic  5.41 us (3%)
  local copies, waits for them, and re-layouts  4.99 us (3%)
    pallas_call x1, Pallas kernels, exchange(): pl.pallas_call(functools.partial(exchange_body, src_count, vol_count, fur...  149 us
    pallas_call x1, Pallas kernels, smooth(): pl.pallas_call(functools.partial(smooth_body, src_count, vol_count), in_s...  13.1 us
    pallas_call x1, Pallas kernels, reduce(): pl.pallas_call(functools.partial(reduce_body, firsts), grid=(channels //...  11 us

profile of v6, /device:TPU:3, one launch (start us, length us, event | category | flops | bytes accessed | tf_op | source)
XLA Modules:
  0.0 184.4 jit_solution(5077646523685792181)
XLA Ops:
  0.0 0.8 select_reduce_fusion.5
  0.8 0.8 select_reduce_fusion.1
  1.6 0.2 convert_reduce_fusion.2
  1.8 0.2 convert_reduce_fusion.1
  2.0 0.1 convert_reduce_fusion
  2.2 0.7 fusion.11
  2.9 0.1 select_reduce_fusion.2
  3.0 0.1 convert_element_type.34
  3.1 0.2 select_reduce_fusion
  3.3 0.1 select_reduce_fusion.4
  3.5 0.1 convert_element_type.35
  3.7 0.6 tile.16.refs_1_
  4.3 0.1 tile.18
  4.4 0.6 pad.12.refs_2_
  5.0 1.5 fusion.1.refs_3_
  6.5 149.2 %shard_map.64 = (bf16[32,9,16,512]{3,2,1,0:T(8,128)(2,1)}, bf16[32,16,128]{2,1,0:T(8,128)(2,1)S(1)}, bf16[32,9,16,512]{3,2,1,0:T(8,128)(2,1)}) custom-call(s32[8,128]{1,0:T(8,128)} %copy-done, bf16[4,16,128]{2,1,0:T(8,128)(2,1)} %tile.16.refs_1_, bf16[16,128]{1,0:T(8,128)(2,1)} %pad.12.refs_2_, bf16[32,16,128]{2,1,0:T(8,128)(2,1)} %fusion.1.refs_3_, ...), custom_call_target="tpu_custom_call" | custom-call | tf_op jit(solution)/shard_map/pallas_call | solution.py:343
  155.7 0.6 slice_reduce_fusion
  157.0 11.0 %shard_map.65 = f32[2,32,512]{2,1,0:T(8,128)S(1)} custom-call(bf16[32,16,128]{2,1,0:T(8,128)(2,1)S(1)} %get-tuple-element.69.notes_ref, bf16[32,9,16,512]{3,2,1,0:T(8,128)(2,1)} %get-tuple-element.70.refs_0_, bf16[32,9,16,512]{3,2,1,0:T(8,128)(2,1)} %get-tuple-element.71.refs_1_, bf16[4,36,32,512]{3,2,1,0:T(8,128)(2,1)} %bitcast.97), custom_call_target="tpu_custom_call" | custom-call | tf_op jit(solution)/shard_map/pallas_call | solution.py:396
  168.0 0.2 copy.11
  168.2 0.6 reshape.527
  168.8 0.9 copy.14
  169.7 1.0 reshape.529
  170.7 13.1 %shard_map.66 = f32[2,8,16,128]{3,2,1,0:T(8,128)S(1)} custom-call(f32[4,8,8,128]{3,2,1,0:T(8,128)S(1)} %bitcast.96), custom_call_target="tpu_custom_call" | custom-call | tf_op jit(solution)/shard_map/pallas_call | solution.py:528
  183.8 0.7 copy.24
  (19 shorter events, 0.3 us)
Async XLA Ops:
  3.5 3.0 %copy-start = (s32[8,128]{1,0:T(8,128)}, s32[8,128]{1,0:T(8,128)S(1)}, u32[]{:S(2)}) copy-start(s32[8,128]{1,0:T(8,128)S(1)} %scatter.14.refs_0_) | copy-start | bytes 12292

commit v7 on v6

--- a/solution.py
+++ b/solution.py
@@ -249,7 +249,7 @@
 
     if further:
         send_rest(my_src, code_row(codes_ref[my_src], 0, SPILL), SPILL, spill_out.at[my_src])
-        first, second = vol_count // 2, vol_count * 3 // 4
+        first, second = vol_count * 3 // 8, vol_count * 7 // 8
         send_turns(0, first)
         near_codes().wait_recv()
         near_copy().wait_recv()

time: 187 us -> 185 us (0.989)
    pallas_call x1, Pallas kernels: 149 us -> 146 us  [exchange(): pl.pallas_call(functools.partial(exchange_body, src_count, vol_count, fur...]
where the time goes in v7:
time: 185 us; the launch traced here: 183 us
  Pallas kernels  172 us (93%)
  other arithmetic  5.41 us (3%)
  local copies, waits for them, and re-layouts  4.99 us (3%)
    pallas_call x1, Pallas kernels, exchange(): pl.pallas_call(functools.partial(exchange_body, src_count, vol_count, fur...  146 us
    pallas_call x1, Pallas kernels, smooth(): pl.pallas_call(functools.partial(smooth_body, src_count, vol_count), in_s...  14.5 us
    pallas_call x1, Pallas kernels, reduce(): pl.pallas_call(functools.partial(reduce_body, firsts), grid=(channels //...  11 us

profile of v7, /device:TPU:3, one launch (start us, length us, event | category | flops | bytes accessed | tf_op | source)
XLA Modules:
  0.0 182.9 jit_solution(10951663953477571019)
XLA Ops:
  0.0 0.8 select_reduce_fusion.5
  0.8 0.8 select_reduce_fusion.1
  1.6 0.2 convert_reduce_fusion.2
  1.8 0.2 convert_reduce_fusion.1
  2.0 0.1 convert_reduce_fusion
  2.2 0.7 fusion.11
  2.9 0.1 select_reduce_fusion.2
  3.0 0.1 convert_element_type.34
  3.1 0.2 select_reduce_fusion
  3.3 0.1 select_reduce_fusion.4
  3.5 0.1 convert_element_type.35
  3.7 0.6 tile.16.refs_1_
  4.3 0.1 tile.18
  4.4 0.6 pad.12.refs_2_
  5.0 1.5 fusion.1.refs_3_
  6.5 146.2 %shard_map.64 = (bf16[32,9,16,512]{3,2,1,0:T(8,128)(2,1)}, bf16[32,16,128]{2,1,0:T(8,128)(2,1)S(1)}, bf16[32,9,16,512]{3,2,1,0:T(8,128)(2,1)}) custom-call(s32[8,128]{1,0:T(8,128)} %copy-done, bf16[4,16,128]{2,1,0:T(8,128)(2,1)} %tile.16.refs_1_, bf16[16,128]{1,0:T(8,128)(2,1)} %pad.12.refs_2_, bf16[32,16,128]{2,1,0:T(8,128)(2,1)} %fusion.1.refs_3_, ...), custom_call_target="tpu_custom_call" | custom-call | tf_op jit(solution)/shard_map/pallas_call | solution.py:343
  152.8 0.6 slice_reduce_fusion
  154.0 11.0 %shard_map.65 = f32[2,32,512]{2,1,0:T(8,128)S(1)} custom-call(bf16[32,16,128]{2,1,0:T(8,128)(2,1)S(1)} %get-tuple-element.69.notes_ref, bf16[32,9,16,512]{3,2,1,0:T(8,128)(2,1)} %get-tuple-element.70.refs_0_, bf16[32,9,16,512]{3,2,1,0:T(8,128)(2,1)} %get-tuple-element.71.refs_1_, bf16[4,36,32,512]{3,2,1,0:T(8,128)(2,1)} %bitcast.97), custom_call_target="tpu_custom_call" | custom-call | tf_op jit(solution)/shard_map/pallas_call | solution.py:396
  165.0 0.2 copy.11
  165.2 0.6 reshape.527
  165.8 0.9 copy.14
  166.7 1.0 reshape.529
  167.7 14.5 %shard_map.66 = f32[2,8,16,128]{3,2,1,0:T(8,128)S(1)} custom-call(f32[4,8,8,128]{3,2,1,0:T(8,128)S(1)} %bitcast.96), custom_call_target="tpu_custom_call" | custom-call | tf_op jit(solution)/shard_map/pallas_call | solution.py:528
  182.3 0.7 copy.24
  (19 shorter events, 0.3 us)
Async XLA Ops:
  3.5 3.0 %copy-start = (s32[8,128]{1,0:T(8,128)}, s32[8,128]{1,0:T(8,128)S(1)}, u32[]{:S(2)}) copy-start(s32[8,128]{1,0:T(8,128)S(1)} %scatter.14.refs_0_) | copy-start | bytes 12292
